TPU v7x, 32 devices: a whole 2x2x4 slice. The times are simulated.
32 devices in a mesh: stream: 8 (over y, x, core), span: 4 (over z).
Axes of the slice: x: 2, y: 2, z: 4, core: 2. Of those that a mesh axis runs over, the one named last changes fastest.
Arguments:
- fluid_pos: float32 [64, 32, 3, 128], P('stream', 'span'), may hold values from 0 to 1
- fluid_vel: float32 [64, 32, 3, 128], P('stream', 'span'), may hold values from -6 to 6
- fluid_mass: float32 [64, 32, 128], P('stream', 'span'), may hold values from 0.5 to 2
- fluid_count: int32 [64, 32], P('stream', 'span'), may hold values from 64 to 128
- clump_center: float32 [16384, 3], P(('stream', 'span')), may hold values from 0 to 1
- clump_vel: float32 [16384, 3], P(('stream', 'span')), may hold values from -6 to 6
- clump_arm: float32 [16384, 3, 128], P(('stream', 'span')), may hold values from -1.8 to 1.8
- margin_device: int32 [16384, 2], P(('stream', 'span')), may hold values from 0 to 31, all different within a row; in each aligned block of 512 rows (0 to 511, 512 to 1023, ...) at most 64 rows name the same one
- margin_block: int32 [16384, 2], P(('stream', 'span')), may hold values from 0 to 63
- margin_offset: float32 [16384, 2, 3], P(('stream', 'span')), may hold values from 0 to 1
- contact_partner: int32 [16384], P(('stream', 'span')), may hold values from 0 to 1023
Outputs:
- fluid_density: float32 [64, 32, 128], P('stream', 'span')
- clump_load: float32 [6, 16384], P(None, ('stream', 'span'))
Inputs may be any that keep to these rules, and one draw needn't show every extreme that they name: `margin_device`: among the 1024 margins of one device's clumps, at most 64 name any one device, and some device is named exactly 64 times; the two margins of a clump name different devices.
All inputs are finite; a program needn't handle non-finite values.
Results may differ from a plain program's by a relative error of at most 0.0001.
Values sent between devices are 32-bit elements; how exact they have to be, the bound alone decides.
A program may use at most 128 MiB of HBM per device.

v0:
```python
import jax
import jax.numpy as jnp
from jax import lax
from jax.sharding import PartitionSpec as P

H_SQ = 0.25
SIG_SQ = 0.5
DENS = 0.03125
DRAG = 0.002
STIFF = 0.005


def extended(cells, sides, width):
    for axis, dim in sides:
        count = lax.axis_size(axis)
        ends = count - 1
        head = lax.slice_in_dim(cells, 0, width, axis=dim)
        tail = lax.slice_in_dim(cells, cells.shape[dim] - width, cells.shape[dim], axis=dim)
        cells = jnp.concatenate(
            [
                lax.ppermute(tail, axis, [(i, (i + 1) % count) for i in range(ends)]),
                cells,
                lax.ppermute(head, axis, [((i + 1) % count, i) for i in range(ends)]),
            ],
            axis=dim,
        )
    return cells


def shifted(array, axis, by):
    peers = lax.axis_size(axis)
    return lax.ppermute(array, axis, [(i, (i + by) % peers) for i in range(peers)])


def particle_mask(fluid_count, width):
    lanes = jnp.arange(width, dtype=jnp.int32)
    return (lanes[None, None, :] < fluid_count[..., None]).astype(jnp.float32)


def pair_sum(center, neigh, shift_x, shift_y):
    delta_x = center[:, 0, :, None] - neigh[:, 0, None, :] - shift_x
    delta_y = center[:, 1, :, None] - neigh[:, 1, None, :] - shift_y
    delta_z = center[:, 2, :, None] - neigh[:, 2, None, :]
    kernel = jnp.exp(-(delta_x * delta_x + delta_y * delta_y + delta_z * delta_z) / H_SQ)
    return jnp.sum(kernel * neigh[:, 3, None, :], axis=2)


def tile_force(pos, amp, offset, arm, velocity):
    spot = offset[:, None] + arm
    delta = pos[:, :, None] - spot[:, None, :]
    kernel = jnp.exp(-jnp.sum(delta * delta, axis=0) / H_SQ)
    acc = jnp.dot(amp, kernel, precision=lax.Precision.HIGHEST)
    return DRAG * (acc[:3] - velocity[:, None] * acc[3][None, :])


def contact_force(mine, other):
    delta = mine[:, :, None] - other[:, None, :]
    kernel = jnp.exp(-jnp.sum(delta * delta, axis=0) / SIG_SQ)
    pulled = jnp.dot(other, kernel.T, precision=lax.Precision.HIGHEST)
    return STIFF * (mine * jnp.sum(kernel, axis=1)[None, :] - pulled)


def body(
    fluid_pos,
    fluid_vel,
    fluid_mass,
    fluid_count,
    clump_center,
    clump_vel,
    clump_arm,
    margin_device,
    margin_block,
    margin_offset,
    contact_partner,
):
    rows_x, rows_y, width = fluid_mass.shape
    live = particle_mask(fluid_count, width)
    packed = jnp.concatenate([fluid_pos, (live * fluid_mass)[:, :, None, :]], axis=2)
    padded = extended(packed, (("stream", 0), ("span", 1)), 1)
    center_rows = padded[1:-1, 1:-1]
    lines = (padded[0:rows_x], padded[1 : rows_x + 1], padded[2 : rows_x + 2])

    def one_row(item):
        center, line_lo, line_mid, line_hi = item
        total = jnp.zeros((rows_y, width), jnp.float32)
        for step_x, line in ((-1, line_lo), (0, line_mid), (1, line_hi)):
            for step_y in (-1, 0, 1):
                total = total + pair_sum(
                    center, line[1 + step_y : 1 + step_y + rows_y], float(step_x), float(step_y)
                )
        return total

    sums = lax.map(one_row, (center_rows, lines[0], lines[1], lines[2]), batch_size=min(rows_x, 8))
    fluid_density = DENS * (fluid_mass + sums)
    weight = live * fluid_mass / fluid_density
    amp = jnp.concatenate([fluid_vel * weight[:, :, None, :], weight[:, :, None, :]], axis=2)
    pos_table = fluid_pos.reshape(rows_x * rows_y, 3, width)
    amp_table = amp.reshape(rows_x * rows_y, 4, width)
    clumps = clump_arm.shape[0]
    spheres = clump_arm.shape[2]
    devices = lax.axis_size(("stream", "span"))
    capacity = 4 * clumps // devices
    entries = 2 * clumps
    slots_all = devices * capacity
    target = margin_device.reshape(entries)
    onehot = (target[:, None] == jnp.arange(devices, dtype=jnp.int32)[None, :]).astype(jnp.float32)
    order = jnp.arange(entries, dtype=jnp.int32)
    lower = (order[:, None] > order[None, :]).astype(jnp.float32)
    before = jnp.dot(lower, onehot, precision=lax.Precision.HIGHEST)
    rank = jnp.sum(before * onehot, axis=1).astype(jnp.int32)
    slot = target * capacity + rank
    slot_ids = jnp.arange(slots_all, dtype=jnp.int32)
    matches = slot[None, :] == slot_ids[:, None]
    filled = jnp.any(matches, axis=1)
    source = jnp.sum(jnp.where(matches, order[None, :], 0), axis=1)
    keep = filled.astype(jnp.float32)
    source_clump = source // 2
    arm_buf = (clump_arm[source_clump] * keep[:, None, None]).reshape(devices, capacity, 3, spheres)
    head_rows = (
        jnp.concatenate(
            [margin_offset.reshape(entries, 3)[source], clump_vel[source_clump]], axis=1
        )
        * keep[:, None]
    )
    head_buf = head_rows.reshape(devices, capacity, 6)
    block_buf = jnp.where(filled, margin_block.reshape(entries)[source], 0).reshape(
        devices, capacity
    )
    arms = lax.all_to_all(arm_buf, ("stream", "span"), split_axis=0, concat_axis=0, tiled=True)
    heads = lax.all_to_all(head_buf, ("stream", "span"), split_axis=0, concat_axis=0, tiled=True)
    blocks = lax.all_to_all(block_buf, ("stream", "span"), split_axis=0, concat_axis=0, tiled=True)
    leading = arms.shape[:2]
    flat_arm = arms.reshape((-1, 3, spheres))
    flat_head = heads.reshape((-1, 6))
    flat_block = blocks.reshape((-1,))
    pos_tiles = pos_table[flat_block]
    amp_tiles = amp_table[flat_block]

    def one_slot(item):
        pos, ampl, arm, head = item
        force = tile_force(pos, ampl, head[:3], arm, head[3:])
        return jnp.concatenate(
            [jnp.sum(force, axis=1), jnp.sum(jnp.cross(arm, force, axis=0), axis=1)]
        )

    results = lax.map(
        one_slot,
        (pos_tiles, amp_tiles, flat_arm, flat_head),
        batch_size=min(flat_block.shape[0], 128),
    )
    returned = lax.all_to_all(
        results.reshape(leading + results.shape[1:]),
        ("stream", "span"),
        split_axis=0,
        concat_axis=0,
        tiled=True,
    )
    returned_flat = returned.reshape((devices * capacity,) + returned.shape[2:])
    picked = returned_flat[slot]
    fluid_part = jnp.sum(picked.reshape((clumps, 2) + picked.shape[1:]), axis=1)
    world = clump_center[:, :, None] + clump_arm
    following = shifted(world, ("stream", "span"), devices - 1)
    candidates = jnp.concatenate([world, following], axis=0)
    partner_pos = candidates[contact_partner]
    contact = lax.map(
        lambda pair: contact_force(pair[0], pair[1]),
        (world, partner_pos),
        batch_size=min(clumps, 128),
    )
    contact_load = jnp.concatenate(
        [jnp.sum(contact, axis=2), jnp.sum(jnp.cross(clump_arm, contact, axis=1), axis=2)], axis=1
    )
    loads = fluid_part + contact_load
    return (fluid_density, loads.T)


def solution(mesh):
    in_specs = (
        P("stream", "span", None, None),
        P("stream", "span", None, None),
        P("stream", "span", None),
        P("stream", "span"),
        P(("stream", "span"), None),
        P(("stream", "span"), None),
        P(("stream", "span"), None, None),
        P(("stream", "span"), None),
        P(("stream", "span"), None),
        P(("stream", "span"), None, None),
        P(("stream", "span")),
    )
    out_specs = (P("stream", "span", None), P(None, ("stream", "span")))
    return jax.shard_map(body, mesh=mesh, in_specs=in_specs, out_specs=out_specs, check_vma=False)
```

profile of v0, /device:TPU:0, one launch (start us, length us, event | category | flops | bytes accessed | tf_op | source)
XLA Modules:
  0.0 714.8 jit_solution(7009478013456178354)
XLA Ops:
  21.6 8.8 %all-to-all-start = ((s32[32,1,64]{2,1,0:T(1,128)}), s32[32,1,64]{2,1,0:T(1,128)}, u32[]{:S(2)}, u32[]{:S(2)}) async-start(s32[32,1,64]{2,1,0:T(1,128)} %select_n.80), calls=%async_computation | async-start | bytes 32768 | tf_op jit(solution)/shard_map/all_to_all | solution.py:131
  49.0 16.5 %gather_fusion.5 = f32[2048,3,128]{2,0,1:T(8,128)} fusion(f32[512,3,128]{2,0,1:T(8,128)S(1)} %copy-done.1, s32[2048]{0:T(1024)S(1)} %broadcast_clamp_fusion), kind=kCustom, calls=%fused_computation.5 | custom fusion | bytes 6299648 | tf_op jit(solution)/shard_map/gather | solution.py:118
  81.8 15.4 %gather_fusion.2 = f32[2048,3,128]{2,1,0:T(4,128)} fusion(f32[64,3,128]{2,1,0:T(4,128)S(1)} %copy.193, s32[2048]{0:T(1024)S(1)} %broadcast_clamp_fusion.1), kind=kCustom, calls=%fused_computation.2 | custom fusion | bytes 6299648 | tf_op jit(solution)/shard_map/gather | solution.py:136
  109.9 13.2 %multiply_reduce_fusion.10 = (f32[8,8,128]{2,1,0:T(8,128)S(1)}, f32[8,8,128]{2,1,0:T(8,128)S(1)}, f32[8,8,128]{2,1,0:T(8,128)S(1)}, f32[8,8,128]{2,1,0:T(8,128)S(1)}) fusion(f32[8,8,128]{2,1,0:T(8,128)S(1)} %get-tuple-element.182, f32[8,8,128]{2,1,0:T(8,128)S(1)} %get-tuple-element.183, f32[8,8,128]{2,1,0:T(8,128)S(1)} %get-tuple-element.202, ...), kind=kLoop, calls=%fused_computation.56 | loop fusion | flops 57638912 | bytes 753664 | tf_op jit(solution)/shard_map/while/body/eval_jaxpr/vmap()/reduce_sum | solution.py:45
  123.2 13.1 %multiply_reduce_fusion.9 = (f32[8,8,128]{2,1,0:T(8,128)S(1)}, f32[8,8,128]{2,1,0:T(8,128)S(1)}, f32[8,8,128]{2,1,0:T(8,128)S(1)}, f32[8,8,128]{2,1,0:T(8,128)S(1)}) fusion(f32[8,8,128]{2,1,0:T(8,128)S(1)} %get-tuple-element.193, f32[8,8,128]{2,1,0:T(8,128)S(1)} %get-tuple-element.191, f32[8,8,128]{2,1,0:T(8,128)S(1)} %get-tuple-element.192, ...), kind=kLoop, calls=%fused_computation.55 | loop fusion | flops 55541760 | bytes 753664 | tf_op jit(solution)/shard_map/while/body/eval_jaxpr/vmap()/reduce_sum | solution.py:45
  137.1 15.3 %gather_fusion.1 = f32[2048,4,128]{2,1,0:T(4,128)} fusion(f32[64,4,128]{2,1,0:T(4,128)S(1)} %pad_maximum_fusion.2, s32[2048]{0:T(1024)S(1)} %broadcast_clamp_fusion.1), kind=kCustom, calls=%fused_computation.1 | custom fusion | bytes 8396800 | tf_op jit(solution)/shard_map/gather | solution.py:137
  167.4 125.2 %while.25 = (s32[]{:T(128)}, f32[4,128,3,128]{3,2,1,0:T(4,128)}, f32[4,128,3,128]{3,2,1,0:T(4,128)S(1)}, f32[4,128,3,128]{3,2,1,0:T(4,128)S(1)}, s32[]{:T(128)}) while((s32[]{:T(128)}, f32[4,128,3,128]{3,2,1,0:T(4,128)}, f32[4,128,3,128]{3,2,1,0:T(4,128)S(1)}, f32[4,128,3,128]{3,2,1,0:T(4,128)S(1)}, s32[]{:T(128)}) %tuple.111), condition=%wide.region_21.22_spmd, body=%wide.region_18.21_spmd.sunk | while | flops 102891520 | bytes 60818524 | solution.py:165
  167.7 11.5 %multiply_reduce_fusion.14 = f32[128,128,128]{2,1,0:T(8,128)} fusion(f32[128,3,128]{2,1,0:T(4,128)S(1)} %get-tuple-element.283, f32[128,3,128]{2,1,0:T(4,128)S(1)} %get-tuple-element.284), kind=kLoop, calls=%fused_computation.32.clone.1 | loop fusion | flops 16777216 | bytes 8781824 | tf_op jit(solution)/shard_map/while/body/eval_jaxpr/vmap()/reduce_sum | solution.py:58
  185.0 13.8 %fusion.47 = f32[4,128,3,128]{3,2,1,0:T(4,128)} fusion(f32[4,128,3,128]{3,2,1,0:T(4,128)} %get-tuple-element.315, s32[]{:T(128)} %get-tuple-element.314, f32[128,128,128]{2,1,0:T(8,128)S(1)} %copy-done, f32[128,128]{1,0:T(8,128)S(1)} %fusion.46, f32[4,128,3,128]{3,2,1,0:T(4,128)S(1)} %get-tuple-element.321, ...), kind=kOutput, calls=%fused_computation.40.clone.1 | convolution fusion | flops 79839232 | bytes 9241600 | tf_op jit(solution)/shard_map/while/body/eval_jaxpr/vmap()/dot_general | solution.py:59
  198.9 11.5 %multiply_reduce_fusion.14 = f32[128,128,128]{2,1,0:T(8,128)} fusion(f32[128,3,128]{2,1,0:T(4,128)S(1)} %get-tuple-element.283, f32[128,3,128]{2,1,0:T(4,128)S(1)} %get-tuple-element.284), kind=kLoop, calls=%fused_computation.32.clone.1 | loop fusion | flops 16777216 | bytes 8781824 | tf_op jit(solution)/shard_map/while/body/eval_jaxpr/vmap()/reduce_sum | solution.py:58
  216.3 13.8 %fusion.47 = f32[4,128,3,128]{3,2,1,0:T(4,128)} fusion(f32[4,128,3,128]{3,2,1,0:T(4,128)} %get-tuple-element.315, s32[]{:T(128)} %get-tuple-element.314, f32[128,128,128]{2,1,0:T(8,128)S(1)} %copy-done, f32[128,128]{1,0:T(8,128)S(1)} %fusion.46, f32[4,128,3,128]{3,2,1,0:T(4,128)S(1)} %get-tuple-element.321, ...), kind=kOutput, calls=%fused_computation.40.clone.1 | convolution fusion | flops 79839232 | bytes 9241600 | tf_op jit(solution)/shard_map/while/body/eval_jaxpr/vmap()/dot_general | solution.py:59
  230.2 11.5 %multiply_reduce_fusion.14 = f32[128,128,128]{2,1,0:T(8,128)} fusion(f32[128,3,128]{2,1,0:T(4,128)S(1)} %get-tuple-element.283, f32[128,3,128]{2,1,0:T(4,128)S(1)} %get-tuple-element.284), kind=kLoop, calls=%fused_computation.32.clone.1 | loop fusion | flops 16777216 | bytes 8781824 | tf_op jit(solution)/shard_map/while/body/eval_jaxpr/vmap()/reduce_sum | solution.py:58
  247.5 13.8 %fusion.47 = f32[4,128,3,128]{3,2,1,0:T(4,128)} fusion(f32[4,128,3,128]{3,2,1,0:T(4,128)} %get-tuple-element.315, s32[]{:T(128)} %get-tuple-element.314, f32[128,128,128]{2,1,0:T(8,128)S(1)} %copy-done, f32[128,128]{1,0:T(8,128)S(1)} %fusion.46, f32[4,128,3,128]{3,2,1,0:T(4,128)S(1)} %get-tuple-element.321, ...), kind=kOutput, calls=%fused_computation.40.clone.1 | convolution fusion | flops 79839232 | bytes 9241600 | tf_op jit(solution)/shard_map/while/body/eval_jaxpr/vmap()/dot_general | solution.py:59
  261.4 11.5 %multiply_reduce_fusion.14 = f32[128,128,128]{2,1,0:T(8,128)} fusion(f32[128,3,128]{2,1,0:T(4,128)S(1)} %get-tuple-element.283, f32[128,3,128]{2,1,0:T(4,128)S(1)} %get-tuple-element.284), kind=kLoop, calls=%fused_computation.32.clone.1 | loop fusion | flops 16777216 | bytes 8781824 | tf_op jit(solution)/shard_map/while/body/eval_jaxpr/vmap()/reduce_sum | solution.py:58
  278.7 13.8 %fusion.47 = f32[4,128,3,128]{3,2,1,0:T(4,128)} fusion(f32[4,128,3,128]{3,2,1,0:T(4,128)} %get-tuple-element.315, s32[]{:T(128)} %get-tuple-element.314, f32[128,128,128]{2,1,0:T(8,128)S(1)} %copy-done, f32[128,128]{1,0:T(8,128)S(1)} %fusion.46, f32[4,128,3,128]{3,2,1,0:T(4,128)S(1)} %get-tuple-element.321, ...), kind=kOutput, calls=%fused_computation.40.clone.1 | convolution fusion | flops 79839232 | bytes 9241600 | tf_op jit(solution)/shard_map/while/body/eval_jaxpr/vmap()/dot_general | solution.py:59
  297.8 397.3 %while.24 = (s32[]{:T(128)}, f32[16,128,6]{1,0,2:T(8,128)S(1)}, f32[16,128,4,128]{3,2,1,0:T(4,128)}, f32[16,128,3,128]{3,2,1,0:T(4,128)}, f32[16,128,6]{1,0,2:T(...) while((s32[]{:T(128)}, f32[16,128,6]{1,0,2:T(8,128)S(1)}, ...), condition=%wide.region_16.17_spmd, body=%wide.region_12.0_spmd.sunk | while | flops 122175488 | bytes 20687464 | solution.py:146
  300.1 11.5 %multiply_reduce_fusion.13 = f32[128,128,128]{2,1,0:T(8,128)} fusion(f32[128,3,128]{2,1,0:T(4,128)S(1)} %copy.259, f32[128,3,128]{2,1,0:T(4,128)S(1)} %dynamic-slice_bitcast_fusion.9), kind=kLoop, calls=%fused_computation.8.clone.1 | loop fusion | flops 16777216 | bytes 8781824 | tf_op jit(solution)/shard_map/while/body/eval_jaxpr/vmap()/reduce_sum | solution.py:51
  311.6 9.5 %fusion.44 = f32[128,4,128]{2,1,0:T(4,128)S(1)} fusion(f32[128,128,128]{2,1,0:T(8,128)} %multiply_reduce_fusion.13, f32[16,128,4,128]{3,2,1,0:T(4,128)} %get-tuple-element.303, s32[]{:T(128)} %get-tuple-element.293), kind=kOutput, calls=%fused_computation.9.clone.1 | convolution fusion | flops 104857600 | bytes 8913408 | tf_op jit(solution)/shard_map/while/body/eval_jaxpr/vmap()/dot_general | solution.py:52
  324.9 11.5 %multiply_reduce_fusion.13 = f32[128,128,128]{2,1,0:T(8,128)} fusion(f32[128,3,128]{2,1,0:T(4,128)S(1)} %copy.259, f32[128,3,128]{2,1,0:T(4,128)S(1)} %dynamic-slice_bitcast_fusion.9), kind=kLoop, calls=%fused_computation.8.clone.1 | loop fusion | flops 16777216 | bytes 8781824 | tf_op jit(solution)/shard_map/while/body/eval_jaxpr/vmap()/reduce_sum | solution.py:51
  336.4 9.5 %fusion.44 = f32[128,4,128]{2,1,0:T(4,128)S(1)} fusion(f32[128,128,128]{2,1,0:T(8,128)} %multiply_reduce_fusion.13, f32[16,128,4,128]{3,2,1,0:T(4,128)} %get-tuple-element.303, s32[]{:T(128)} %get-tuple-element.293), kind=kOutput, calls=%fused_computation.9.clone.1 | convolution fusion | flops 104857600 | bytes 8913408 | tf_op jit(solution)/shard_map/while/body/eval_jaxpr/vmap()/dot_general | solution.py:52
  349.7 11.5 %multiply_reduce_fusion.13 = f32[128,128,128]{2,1,0:T(8,128)} fusion(f32[128,3,128]{2,1,0:T(4,128)S(1)} %copy.259, f32[128,3,128]{2,1,0:T(4,128)S(1)} %dynamic-slice_bitcast_fusion.9), kind=kLoop, calls=%fused_computation.8.clone.1 | loop fusion | flops 16777216 | bytes 8781824 | tf_op jit(solution)/shard_map/while/body/eval_jaxpr/vmap()/reduce_sum | solution.py:51
  361.3 9.5 %fusion.44 = f32[128,4,128]{2,1,0:T(4,128)S(1)} fusion(f32[128,128,128]{2,1,0:T(8,128)} %multiply_reduce_fusion.13, f32[16,128,4,128]{3,2,1,0:T(4,128)} %get-tuple-element.303, s32[]{:T(128)} %get-tuple-element.293), kind=kOutput, calls=%fused_computation.9.clone.1 | convolution fusion | flops 104857600 | bytes 8913408 | tf_op jit(solution)/shard_map/while/body/eval_jaxpr/vmap()/dot_general | solution.py:52
  374.6 11.5 %multiply_reduce_fusion.13 = f32[128,128,128]{2,1,0:T(8,128)} fusion(f32[128,3,128]{2,1,0:T(4,128)S(1)} %copy.259, f32[128,3,128]{2,1,0:T(4,128)S(1)} %dynamic-slice_bitcast_fusion.9), kind=kLoop, calls=%fused_computation.8.clone.1 | loop fusion | flops 16777216 | bytes 8781824 | tf_op jit(solution)/shard_map/while/body/eval_jaxpr/vmap()/reduce_sum | solution.py:51
  386.1 9.5 %fusion.44 = f32[128,4,128]{2,1,0:T(4,128)S(1)} fusion(f32[128,128,128]{2,1,0:T(8,128)} %multiply_reduce_fusion.13, f32[16,128,4,128]{3,2,1,0:T(4,128)} %get-tuple-element.303, s32[]{:T(128)} %get-tuple-element.293), kind=kOutput, calls=%fused_computation.9.clone.1 | convolution fusion | flops 104857600 | bytes 8913408 | tf_op jit(solution)/shard_map/while/body/eval_jaxpr/vmap()/dot_general | solution.py:52
  399.4 11.5 %multiply_reduce_fusion.13 = f32[128,128,128]{2,1,0:T(8,128)} fusion(f32[128,3,128]{2,1,0:T(4,128)S(1)} %copy.259, f32[128,3,128]{2,1,0:T(4,128)S(1)} %dynamic-slice_bitcast_fusion.9), kind=kLoop, calls=%fused_computation.8.clone.1 | loop fusion | flops 16777216 | bytes 8781824 | tf_op jit(solution)/shard_map/while/body/eval_jaxpr/vmap()/reduce_sum | solution.py:51
  410.9 9.5 %fusion.44 = f32[128,4,128]{2,1,0:T(4,128)S(1)} fusion(f32[128,128,128]{2,1,0:T(8,128)} %multiply_reduce_fusion.13, f32[16,128,4,128]{3,2,1,0:T(4,128)} %get-tuple-element.303, s32[]{:T(128)} %get-tuple-element.293), kind=kOutput, calls=%fused_computation.9.clone.1 | convolution fusion | flops 104857600 | bytes 8913408 | tf_op jit(solution)/shard_map/while/body/eval_jaxpr/vmap()/dot_general | solution.py:52
  424.2 11.5 %multiply_reduce_fusion.13 = f32[128,128,128]{2,1,0:T(8,128)} fusion(f32[128,3,128]{2,1,0:T(4,128)S(1)} %copy.259, f32[128,3,128]{2,1,0:T(4,128)S(1)} %dynamic-slice_bitcast_fusion.9), kind=kLoop, calls=%fused_computation.8.clone.1 | loop fusion | flops 16777216 | bytes 8781824 | tf_op jit(solution)/shard_map/while/body/eval_jaxpr/vmap()/reduce_sum | solution.py:51
  435.8 9.5 %fusion.44 = f32[128,4,128]{2,1,0:T(4,128)S(1)} fusion(f32[128,128,128]{2,1,0:T(8,128)} %multiply_reduce_fusion.13, f32[16,128,4,128]{3,2,1,0:T(4,128)} %get-tuple-element.303, s32[]{:T(128)} %get-tuple-element.293), kind=kOutput, calls=%fused_computation.9.clone.1 | convolution fusion | flops 104857600 | bytes 8913408 | tf_op jit(solution)/shard_map/while/body/eval_jaxpr/vmap()/dot_general | solution.py:52
  449.1 11.5 %multiply_reduce_fusion.13 = f32[128,128,128]{2,1,0:T(8,128)} fusion(f32[128,3,128]{2,1,0:T(4,128)S(1)} %copy.259, f32[128,3,128]{2,1,0:T(4,128)S(1)} %dynamic-slice_bitcast_fusion.9), kind=kLoop, calls=%fused_computation.8.clone.1 | loop fusion | flops 16777216 | bytes 8781824 | tf_op jit(solution)/shard_map/while/body/eval_jaxpr/vmap()/reduce_sum | solution.py:51
  460.6 9.5 %fusion.44 = f32[128,4,128]{2,1,0:T(4,128)S(1)} fusion(f32[128,128,128]{2,1,0:T(8,128)} %multiply_reduce_fusion.13, f32[16,128,4,128]{3,2,1,0:T(4,128)} %get-tuple-element.303, s32[]{:T(128)} %get-tuple-element.293), kind=kOutput, calls=%fused_computation.9.clone.1 | convolution fusion | flops 104857600 | bytes 8913408 | tf_op jit(solution)/shard_map/while/body/eval_jaxpr/vmap()/dot_general | solution.py:52
  473.9 11.5 %multiply_reduce_fusion.13 = f32[128,128,128]{2,1,0:T(8,128)} fusion(f32[128,3,128]{2,1,0:T(4,128)S(1)} %copy.259, f32[128,3,128]{2,1,0:T(4,128)S(1)} %dynamic-slice_bitcast_fusion.9), kind=kLoop, calls=%fused_computation.8.clone.1 | loop fusion | flops 16777216 | bytes 8781824 | tf_op jit(solution)/shard_map/while/body/eval_jaxpr/vmap()/reduce_sum | solution.py:51
  485.4 9.5 %fusion.44 = f32[128,4,128]{2,1,0:T(4,128)S(1)} fusion(f32[128,128,128]{2,1,0:T(8,128)} %multiply_reduce_fusion.13, f32[16,128,4,128]{3,2,1,0:T(4,128)} %get-tuple-element.303, s32[]{:T(128)} %get-tuple-element.293), kind=kOutput, calls=%fused_computation.9.clone.1 | convolution fusion | flops 104857600 | bytes 8913408 | tf_op jit(solution)/shard_map/while/body/eval_jaxpr/vmap()/dot_general | solution.py:52
  498.7 11.5 %multiply_reduce_fusion.13 = f32[128,128,128]{2,1,0:T(8,128)} fusion(f32[128,3,128]{2,1,0:T(4,128)S(1)} %copy.259, f32[128,3,128]{2,1,0:T(4,128)S(1)} %dynamic-slice_bitcast_fusion.9), kind=kLoop, calls=%fused_computation.8.clone.1 | loop fusion | flops 16777216 | bytes 8781824 | tf_op jit(solution)/shard_map/while/body/eval_jaxpr/vmap()/reduce_sum | solution.py:51
  510.3 9.5 %fusion.44 = f32[128,4,128]{2,1,0:T(4,128)S(1)} fusion(f32[128,128,128]{2,1,0:T(8,128)} %multiply_reduce_fusion.13, f32[16,128,4,128]{3,2,1,0:T(4,128)} %get-tuple-element.303, s32[]{:T(128)} %get-tuple-element.293), kind=kOutput, calls=%fused_computation.9.clone.1 | convolution fusion | flops 104857600 | bytes 8913408 | tf_op jit(solution)/shard_map/while/body/eval_jaxpr/vmap()/dot_general | solution.py:52
  523.6 11.5 %multiply_reduce_fusion.13 = f32[128,128,128]{2,1,0:T(8,128)} fusion(f32[128,3,128]{2,1,0:T(4,128)S(1)} %copy.259, f32[128,3,128]{2,1,0:T(4,128)S(1)} %dynamic-slice_bitcast_fusion.9), kind=kLoop, calls=%fused_computation.8.clone.1 | loop fusion | flops 16777216 | bytes 8781824 | tf_op jit(solution)/shard_map/while/body/eval_jaxpr/vmap()/reduce_sum | solution.py:51
  535.1 9.5 %fusion.44 = f32[128,4,128]{2,1,0:T(4,128)S(1)} fusion(f32[128,128,128]{2,1,0:T(8,128)} %multiply_reduce_fusion.13, f32[16,128,4,128]{3,2,1,0:T(4,128)} %get-tuple-element.303, s32[]{:T(128)} %get-tuple-element.293), kind=kOutput, calls=%fused_computation.9.clone.1 | convolution fusion | flops 104857600 | bytes 8913408 | tf_op jit(solution)/shard_map/while/body/eval_jaxpr/vmap()/dot_general | solution.py:52
  548.4 11.5 %multiply_reduce_fusion.13 = f32[128,128,128]{2,1,0:T(8,128)} fusion(f32[128,3,128]{2,1,0:T(4,128)S(1)} %copy.259, f32[128,3,128]{2,1,0:T(4,128)S(1)} %dynamic-slice_bitcast_fusion.9), kind=kLoop, calls=%fused_computation.8.clone.1 | loop fusion | flops 16777216 | bytes 8781824 | tf_op jit(solution)/shard_map/while/body/eval_jaxpr/vmap()/reduce_sum | solution.py:51
  559.9 9.5 %fusion.44 = f32[128,4,128]{2,1,0:T(4,128)S(1)} fusion(f32[128,128,128]{2,1,0:T(8,128)} %multiply_reduce_fusion.13, f32[16,128,4,128]{3,2,1,0:T(4,128)} %get-tuple-element.303, s32[]{:T(128)} %get-tuple-element.293), kind=kOutput, calls=%fused_computation.9.clone.1 | convolution fusion | flops 104857600 | bytes 8913408 | tf_op jit(solution)/shard_map/while/body/eval_jaxpr/vmap()/dot_general | solution.py:52
  573.2 11.5 %multiply_reduce_fusion.13 = f32[128,128,128]{2,1,0:T(8,128)} fusion(f32[128,3,128]{2,1,0:T(4,128)S(1)} %copy.259, f32[128,3,128]{2,1,0:T(4,128)S(1)} %dynamic-slice_bitcast_fusion.9), kind=kLoop, calls=%fused_computation.8.clone.1 | loop fusion | flops 16777216 | bytes 8781824 | tf_op jit(solution)/shard_map/while/body/eval_jaxpr/vmap()/reduce_sum | solution.py:51
  584.8 9.5 %fusion.44 = f32[128,4,128]{2,1,0:T(4,128)S(1)} fusion(f32[128,128,128]{2,1,0:T(8,128)} %multiply_reduce_fusion.13, f32[16,128,4,128]{3,2,1,0:T(4,128)} %get-tuple-element.303, s32[]{:T(128)} %get-tuple-element.293), kind=kOutput, calls=%fused_computation.9.clone.1 | convolution fusion | flops 104857600 | bytes 8913408 | tf_op jit(solution)/shard_map/while/body/eval_jaxpr/vmap()/dot_general | solution.py:52
  598.1 11.5 %multiply_reduce_fusion.13 = f32[128,128,128]{2,1,0:T(8,128)} fusion(f32[128,3,128]{2,1,0:T(4,128)S(1)} %copy.259, f32[128,3,128]{2,1,0:T(4,128)S(1)} %dynamic-slice_bitcast_fusion.9), kind=kLoop, calls=%fused_computation.8.clone.1 | loop fusion | flops 16777216 | bytes 8781824 | tf_op jit(solution)/shard_map/while/body/eval_jaxpr/vmap()/reduce_sum | solution.py:51
  609.6 9.5 %fusion.44 = f32[128,4,128]{2,1,0:T(4,128)S(1)} fusion(f32[128,128,128]{2,1,0:T(8,128)} %multiply_reduce_fusion.13, f32[16,128,4,128]{3,2,1,0:T(4,128)} %get-tuple-element.303, s32[]{:T(128)} %get-tuple-element.293), kind=kOutput, calls=%fused_computation.9.clone.1 | convolution fusion | flops 104857600 | bytes 8913408 | tf_op jit(solution)/shard_map/while/body/eval_jaxpr/vmap()/dot_general | solution.py:52
  622.9 11.5 %multiply_reduce_fusion.13 = f32[128,128,128]{2,1,0:T(8,128)} fusion(f32[128,3,128]{2,1,0:T(4,128)S(1)} %copy.259, f32[128,3,128]{2,1,0:T(4,128)S(1)} %dynamic-slice_bitcast_fusion.9), kind=kLoop, calls=%fused_computation.8.clone.1 | loop fusion | flops 16777216 | bytes 8781824 | tf_op jit(solution)/shard_map/while/body/eval_jaxpr/vmap()/reduce_sum | solution.py:51
  634.4 9.5 %fusion.44 = f32[128,4,128]{2,1,0:T(4,128)S(1)} fusion(f32[128,128,128]{2,1,0:T(8,128)} %multiply_reduce_fusion.13, f32[16,128,4,128]{3,2,1,0:T(4,128)} %get-tuple-element.303, s32[]{:T(128)} %get-tuple-element.293), kind=kOutput, calls=%fused_computation.9.clone.1 | convolution fusion | flops 104857600 | bytes 8913408 | tf_op jit(solution)/shard_map/while/body/eval_jaxpr/vmap()/dot_general | solution.py:52
  647.7 11.5 %multiply_reduce_fusion.13 = f32[128,128,128]{2,1,0:T(8,128)} fusion(f32[128,3,128]{2,1,0:T(4,128)S(1)} %copy.259, f32[128,3,128]{2,1,0:T(4,128)S(1)} %dynamic-slice_bitcast_fusion.9), kind=kLoop, calls=%fused_computation.8.clone.1 | loop fusion | flops 16777216 | bytes 8781824 | tf_op jit(solution)/shard_map/while/body/eval_jaxpr/vmap()/reduce_sum | solution.py:51
  659.2 9.5 %fusion.44 = f32[128,4,128]{2,1,0:T(4,128)S(1)} fusion(f32[128,128,128]{2,1,0:T(8,128)} %multiply_reduce_fusion.13, f32[16,128,4,128]{3,2,1,0:T(4,128)} %get-tuple-element.303, s32[]{:T(128)} %get-tuple-element.293), kind=kOutput, calls=%fused_computation.9.clone.1 | convolution fusion | flops 104857600 | bytes 8913408 | tf_op jit(solution)/shard_map/while/body/eval_jaxpr/vmap()/dot_general | solution.py:52
  672.5 11.5 %multiply_reduce_fusion.13 = f32[128,128,128]{2,1,0:T(8,128)} fusion(f32[128,3,128]{2,1,0:T(4,128)S(1)} %copy.259, f32[128,3,128]{2,1,0:T(4,128)S(1)} %dynamic-slice_bitcast_fusion.9), kind=kLoop, calls=%fused_computation.8.clone.1 | loop fusion | flops 16777216 | bytes 8781824 | tf_op jit(solution)/shard_map/while/body/eval_jaxpr/vmap()/reduce_sum | solution.py:51
  684.1 9.5 %fusion.44 = f32[128,4,128]{2,1,0:T(4,128)S(1)} fusion(f32[128,128,128]{2,1,0:T(8,128)} %multiply_reduce_fusion.13, f32[16,128,4,128]{3,2,1,0:T(4,128)} %get-tuple-element.303, s32[]{:T(128)} %get-tuple-element.293), kind=kOutput, calls=%fused_computation.9.clone.1 | convolution fusion | flops 104857600 | bytes 8913408 | tf_op jit(solution)/shard_map/while/body/eval_jaxpr/vmap()/dot_general | solution.py:52
  (368 shorter events, 191.3 us)
Async XLA Ops:
  2.8 94.4 %collective-permute-start = (f32[1,8,4,128]{3,1,2,0:T(8,128)}, f32[1,8,4,128]{3,1,2,0:T(8,128)}, u32[]{:S(2)}, u32[]{:S(2)}) collective-permute-start(f32[1,8,4,128]{3,1,2,0:T(8,128)} %get-tuple-element.198), channel_id=1, source_target_pairs={{0,4},{4,8},{8,12},{12,16},{16,20},{20,24},{24,28},{1,5},{5,9},{9,... | collective-permute-start | bytes 49160 | tf_op jit(solution)/shard_map/ppermute | solution.py:21
  5.7 91.5 %collective-permute-start.1 = (f32[1,8,4,128]{3,1,2,0:T(8,128)}, f32[1,8,4,128]{3,1,2,0:T(8,128)S(1)}, u32[]{:S(2)}, u32[]{:S(2)}) collective-permute-start(f32[1,8,4,128]{3,1,2,0:T(8,128)} %get-tuple-element.199), channel_id=1, source_target_pairs={{4,0},{8,4},{12,8},{16,12},{20,16},{24,20},{28,24},{5,1},{9,5},{13... | collective-permute-start | bytes 49160 | tf_op jit(solution)/shard_map/ppermute | solution.py:23
  12.2 18.1 %copy-start.13 = (f32[512,3]{0,1:T(4,128)S(1)}, f32[512,3]{0,1:T(4,128)}, u32[]{:S(2)}) copy-start(f32[512,3]{0,1:T(4,128)} %param.19) | copy-start | bytes 18436
  12.2 18.3 %copy-start.1 = (f32[512,3,128]{2,0,1:T(8,128)S(1)}, f32[512,3,128]{2,0,1:T(8,128)}, u32[]{:S(2)}) copy-start(f32[512,3,128]{2,0,1:T(8,128)} %param.21) | copy-start | bytes 2359300
  20.8 18.0 %copy-start.3 = (f32[8,8,128]{2,1,0:T(8,128)S(1)}, f32[8,8,128]{2,1,0:T(8,128)}, u32[]{:S(2)}) copy-start(f32[8,8,128]{2,1,0:T(8,128)} %param.17) | copy-start | bytes 98308
  20.8 18.0 %copy-start.5 = (s32[8,8]{1,0:T(8,128)S(1)}, s32[8,8]{1,0:T(8,128)}, u32[]{:S(2)}) copy-start(s32[8,8]{1,0:T(8,128)} %param.18) | copy-start | bytes 772
  20.8 19.9 %copy-start.9 = (s32[512,2]{0,1:T(2,128)S(1)}, s32[512,2]{0,1:T(2,128)}, u32[]{:S(2)}) copy-start(s32[512,2]{0,1:T(2,128)} %param.22) | copy-start | bytes 12292
  20.9 20.5 %copy-start.12 = (f32[512,2,3]{0,1,2:T(2,128)S(1)}, f32[512,2,3]{0,1,2:T(2,128)}, u32[]{:S(2)}) copy-start(f32[512,2,3]{0,1,2:T(2,128)} %param.24) | copy-start | bytes 36868
  21.6 55.5 %all-to-all-start = ((s32[32,1,64]{2,1,0:T(1,128)}), s32[32,1,64]{2,1,0:T(1,128)}, u32[]{:S(2)}, u32[]{:S(2)}) async-start(s32[32,1,64]{2,1,0:T(1,128)} %select_n.80), calls=%async_computation | async-start | bytes 32768 | tf_op jit(solution)/shard_map/all_to_all | solution.py:131
  33.7 127.1 %collective-permute-start.4 = (f32[512,3,128]{2,0,1:T(8,128)}, f32[512,3,128]{2,0,1:T(8,128)}, u32[]{:S(2)}, u32[]{:S(2)}) collective-permute-start(f32[512,3,128]{2,0,1:T(8,128)} %copy.209), channel_id=1, source_target_pairs={{0,31},{1,0},{2,1},{3,2},{4,3},{5,4},{6,5},{7,6},{8,7},{9,8},{10,9... | collective-permute-start | bytes 2359304 | tf_op jit(solution)/shard_map/ppermute | solution.py:32
  65.6 5.9 copy-start.7
  65.6 6.0 copy-start.10
  65.6 6.3 copy-start.11
  65.6 6.4 copy-start.14
  71.0 5.2 copy-start.2
  77.1 75.3 %all-to-all-start.1 = ((f32[32,1,384]{2,1,0:T(1,128)}), f32[32,1,384]{2,1,0:T(1,128)S(1)}, u32[]{:S(2)}, u32[]{:S(2)}) async-start(f32[32,1,384]{2,1,0:T(1,128)} %reshape.601), calls=%async_computation.1 | async-start | bytes 98304 | tf_op jit(solution)/shard_map/all_to_all | solution.py:130
  81.8 21.9 %copy-start.8 = (f32[8,8,128]{2,1,0:T(8,128)S(1)}, f32[8,8,128]{2,1,0:T(8,128)}, u32[]{:S(2)}) copy-start(f32[8,8,128]{2,1,0:T(8,128)} %fusion.29) | copy-start | bytes 98308
  98.0 10.9 %collective-permute-start.2 = (f32[10,1,4,128]{3,1,2,0:T(1,128)S(1)}, f32[10,1,4,128]{3,1,2,0:T(1,128)S(1)}, u32[]{:S(2)}, u32[]{:S(2)}) collective-permute-start(f32[10,1,4,128]{3,1,2,0:T(1,128)S(1)} %get-tuple-element.189), channel_id=1, source_target_pairs={{0,1},{1,2},{2,3},{4,5},{5,6},{6,7},{8,9},{9,10},{10,11},{12,13},{... | collective-permute-start | bytes 61448 | tf_op jit(solution)/shard_map/ppermute | solution.py:21
  101.6 7.3 %collective-permute-start.3 = (f32[10,1,4,128]{3,1,2,0:T(1,128)S(1)}, f32[10,1,4,128]{3,1,2,0:T(1,128)S(1)}, u32[]{:S(2)}, u32[]{:S(2)}) collective-permute-start(f32[10,1,4,128]{3,1,2,0:T(1,128)S(1)} %get-tuple-element.188), channel_id=1, source_target_pairs={{1,0},{2,1},{3,2},{5,4},{6,5},{7,6},{9,8},{10,9},{11,10},{13,12},{... | collective-permute-start | bytes 61448 | tf_op jit(solution)/shard_map/ppermute | solution.py:23
  123.1 13.1 %copy-start.6 = (s32[8,8]{1,0:T(8,128)S(1)}, s32[8,8]{1,0:T(8,128)}, u32[]{:S(2)}) copy-start(s32[8,8]{1,0:T(8,128)} %param.18) | copy-start | bytes 772
  123.1 13.8 %copy-start.4 = (f32[8,8,3,128]{3,1,2,0:T(8,128)S(1)}, f32[8,8,3,128]{3,1,2,0:T(8,128)}, u32[]{:S(2)}) copy-start(f32[8,8,3,128]{3,1,2,0:T(8,128)} %param.16) | copy-start | bytes 294916
  152.4 141.5 %all-to-all-start.2 = ((f32[32,64,3,128]{3,1,2,0:T(8,128)}), f32[32,64,3,128]{3,1,2,0:T(8,128)}, u32[]{:S(2)}, u32[]{:S(2)}) async-start(f32[32,64,3,128]{3,1,2,0:T(8,128)} %copy_multiply_fusion), calls=%async_computation.2 | async-start | bytes 6291456 | tf_op jit(solution)/shard_map/all_to_all | solution.py:129
  179.2 5.8 copy-start
  210.5 5.8 copy-start
  241.7 5.8 copy-start
  272.9 5.8 copy-start
  696.0 13.2 %all-to-all-start.3 = ((f32[32,1,384]{2,1,0:T(1,128)}), f32[32,1,384]{2,1,0:T(1,128)S(1)}, u32[]{:S(2)}, u32[]{:S(2)}) async-start(f32[32,1,384]{2,1,0:T(1,128)} %reshape.603), calls=%async_computation.3 | async-start | bytes 98304 | tf_op jit(solution)/shard_map/all_to_all | solution.py:151
where the time goes:
time: 717 us; the launch traced here: 715 us
  other arithmetic  334 us (47%)
  matrix products  208 us (29%)
  local copies, waits for them, and re-layouts  126 us (18%)
  starting transfers between devices  38.3 us (5%)
    reduce_sum x16, other arithmetic, tile_force(): kernel = jnp.exp(-jnp.sum(delta * delta, axis=0) / H_SQ)  184 us
    dot_general x16, matrix products, tile_force(): acc = jnp.dot(amp, kernel, precision=lax.Precision.HIGHEST)  152 us
    dot_general x4, matrix products, contact_force(): pulled = jnp.dot(other, kernel.T, precision=lax.Precision.HIGHEST)  55.3 us
    reduce_sum x4, other arithmetic, contact_force(): kernel = jnp.exp(-jnp.sum(delta * delta, axis=0) / SIG_SQ)  46.1 us
    reduce_sum x3, other arithmetic, pair_sum(): return jnp.sum(kernel * neigh[:, 3, None, :], axis=2)  31.5 us
    reduce_sum x4, other arithmetic, contact_force(): return STIFF * (mine * jnp.sum(kernel, axis=1)[None, :] - pulled)  23.1 us
    add x16, other arithmetic, tile_force(): spot = offset[:, None] + arm  16.8 us
    gather x1, local copies, waits for them, and re-layouts, body(): clump_arm[source_clump] * keep[:, None, None]  16.5 us
  transfers between devices with their start and end apart: 9, of which 1 were waited for; matrix products, arithmetic and copies ran while one was open for 36% of the time, Pallas kernels for 0%

commit v1 on v0

v1 whole, which is shorter than its diff:
```python
import functools

import jax
import jax.numpy as jnp
from jax import lax
from jax.experimental import pallas as pl
from jax.experimental.pallas import tpu as pltpu
from jax.sharding import PartitionSpec as P

INV_H = 4.0
INV_SIG = 2.0
DENS = 0.03125
DRAG = 0.002
STIFF = 0.005
AXES = ("stream", "span")
VMEM_BYTES = 58 * 1024 * 1024


def extended(cells, sides, width):
    for axis, dim in sides:
        count = lax.axis_size(axis)
        ends = count - 1
        head = lax.slice_in_dim(cells, 0, width, axis=dim)
        tail = lax.slice_in_dim(cells, cells.shape[dim] - width, cells.shape[dim], axis=dim)
        cells = jnp.concatenate(
            [
                lax.ppermute(tail, axis, [(i, (i + 1) % count) for i in range(ends)]),
                cells,
                lax.ppermute(head, axis, [((i + 1) % count, i) for i in range(ends)]),
            ],
            axis=dim,
        )
    return cells


def split(value):
    high = value.astype(jnp.bfloat16).astype(jnp.float32)
    rest = value - high
    mid = rest.astype(jnp.bfloat16).astype(jnp.float32)
    return high, mid, rest - mid


def near_stack(value):
    a, b, c = split(value)
    return jnp.concatenate([a, a, a, b, b, c], axis=0).astype(jnp.bfloat16)


def far_stack(value):
    a, b, c = split(value)
    return jnp.concatenate([a, b, c, a, b, a], axis=0).astype(jnp.bfloat16)


def near_rows(point, row):
    point = jnp.where(row < 3, point, 0.0)
    norm = jnp.sum(point * point, axis=0, keepdims=True)
    return jnp.where(row == 3, norm, jnp.where(row == 4, 1.0, point))


def far_rows(point, row, scale, extra):
    norm = jnp.sum(point * point, axis=0, keepdims=True)
    last = extra - scale * norm
    return jnp.where(row == 3, -scale, jnp.where(row == 4, last, (2.0 * scale) * point))


def column(row, x, y, z):
    return jnp.where(row == 0, x, jnp.where(row == 1, y, jnp.where(row == 2, z, 0.0)))


def exponents(near, far):
    return lax.dot_general(
        near, far, (((0,), (0,)), ((), ())), preferred_element_type=jnp.float32
    )


def gathered_sum(amp, kernel):
    both = lax.dot_general(
        amp, kernel, (((1,), (1,)), ((), ())), preferred_element_type=jnp.float32
    )
    return both[0:8] + both[8:16]


def amp_stack(value):
    high = value.astype(jnp.bfloat16).astype(jnp.float32)
    return jnp.concatenate([high, value - high], axis=0).astype(jnp.bfloat16)


def density_kernel(rows_x, rows_y, cells_ref, out_ref):
    row = lax.broadcasted_iota(jnp.int32, (8, 128), 0)

    def step(index, carry):
        bx = index // rows_y
        by = index % rows_y
        near = near_stack(near_rows(cells_ref[bx + 1, by + 1], row))
        total = jnp.zeros((128, 128), jnp.float32)
        for step_x in (-1, 0, 1):
            for step_y in (-1, 0, 1):
                cell = cells_ref[bx + 1 + step_x, by + 1 + step_y]
                point = jnp.where(
                    row < 3, cell + column(row, float(step_x), float(step_y), 0.0), 0.0
                )
                far = far_stack(far_rows(point, row, INV_H, cell[3:4]))
                total = total + jnp.exp(exponents(near, far))
        out_ref[pl.ds(index, 1), :] = jnp.sum(total.T, axis=0, keepdims=True)
        return carry

    lax.fori_loop(0, rows_x * rows_y, step, 0)


def contact_kernel(clumps, batch, partner_ref, center_ref, near_ref, out_ref):
    row = lax.broadcasted_iota(jnp.int32, (8, 128), 0)

    def step(index, carry):
        for k in range(batch):
            c = index * batch + k
            p = partner_ref[c]
            shift = column(
                row,
                center_ref[3 * p] - center_ref[3 * c],
                center_ref[3 * p + 1] - center_ref[3 * c + 1],
                center_ref[3 * p + 2] - center_ref[3 * c + 2],
            )
            near = near_stack(near_ref[c])
            point = jnp.where(row < 3, near_ref[p] + shift, 0.0)
            far = far_stack(far_rows(point, row, INV_SIG, 0.0))
            kernel = jnp.exp(exponents(near, far)).astype(jnp.bfloat16)
            amp = amp_stack(jnp.where(row == 3, 1.0, point))
            out_ref[c] = gathered_sum(amp, kernel)
        return carry

    lax.fori_loop(0, clumps // batch, step, 0)


def fluid_kernel(clumps, batch, block_ref, offset_ref, near_ref, table_ref, out_ref):
    row = lax.broadcasted_iota(jnp.int32, (8, 128), 0)

    def step(index, carry):
        for k in range(batch):
            c = index * batch + k
            near = near_stack(near_ref[c])
            fars, amps = [], []
            for m in range(2):
                e = 2 * c + m
                cell = table_ref[block_ref[e]]
                shift = column(
                    row, offset_ref[3 * e], offset_ref[3 * e + 1], offset_ref[3 * e + 2]
                )
                point = jnp.where(row < 3, cell - shift, 0.0)
                fars.append(far_stack(far_rows(point, row, INV_H, 0.0)))
                amps.append(amp_stack(cell))
            far = jnp.concatenate(fars, axis=1)
            amp = jnp.concatenate(amps, axis=1)
            kernel = jnp.exp(exponents(near, far)).astype(jnp.bfloat16)
            out_ref[c] = gathered_sum(amp, kernel)
        return carry

    lax.fori_loop(0, clumps // batch, step, 0)


def call(kernel, shape, scalars, arrays, tiles):
    smem = pl.BlockSpec(memory_space=pltpu.SMEM)
    vmem = pl.BlockSpec(memory_space=pltpu.VMEM)
    return pl.pallas_call(
        kernel,
        out_shape=jax.ShapeDtypeStruct(shape, jnp.float32),
        in_specs=[smem] * len(scalars) + [vmem] * len(arrays),
        out_specs=vmem,
        compiler_params=pltpu.CompilerParams(vmem_limit_bytes=VMEM_BYTES),
        cost_estimate=pl.CostEstimate(
            flops=tiles * 128 * 128 * 128,
            bytes_accessed=4 * sum(a.size for a in arrays),
            transcendentals=tiles * 128 * 128,
        ),
    )(*scalars, *arrays)


def body(
    fluid_pos,
    fluid_vel,
    fluid_mass,
    fluid_count,
    clump_center,
    clump_vel,
    clump_arm,
    margin_device,
    margin_block,
    margin_offset,
    contact_partner,
):
    rows_x, rows_y, width = fluid_mass.shape
    cells = rows_x * rows_y
    clumps = clump_arm.shape[0]
    spheres = clump_arm.shape[2]
    devices = lax.axis_size(AXES)
    back = [(i, (i + devices - 1) % devices) for i in range(devices)]

    lanes = jnp.arange(width, dtype=jnp.int32)
    live = (lanes[None, None, :] < fluid_count[..., None]).astype(jnp.float32)
    live_mass = live * fluid_mass
    centered = fluid_pos - 0.5
    packed = jnp.concatenate([centered, live_mass[:, :, None, :]], axis=2)
    padded = extended(packed, (("stream", 0), ("span", 1)), 1)
    mass = padded[:, :, 3:4]
    log_mass = jnp.where(mass > 0, jnp.log(jnp.maximum(mass, 1e-30)), -1e30)
    padded = jnp.concatenate(
        [padded[:, :, 0:3], log_mass, jnp.zeros(padded.shape[:2] + (4, width), jnp.float32)],
        axis=2,
    )
    sums = call(
        functools.partial(density_kernel, rows_x, rows_y),
        (cells, width),
        (),
        (padded,),
        9 * cells,
    )
    fluid_density = DENS * (fluid_mass + sums.reshape(rows_x, rows_y, width))
    weight = (live_mass / fluid_density)[:, :, None, :]
    table = jnp.concatenate(
        [centered, jnp.zeros_like(weight), fluid_vel * weight, weight], axis=2
    ).reshape(cells, 8, width)
    table = lax.all_gather(table, AXES, axis=0, tiled=True)

    center_next = lax.ppermute(clump_center, AXES, back)
    arm_next = lax.ppermute(clump_arm, AXES, back)
    centers = jnp.concatenate([clump_center, center_next], axis=0).reshape(-1)
    arms = jnp.concatenate([clump_arm, arm_next], axis=0)
    near = jnp.concatenate(
        [
            arms,
            jnp.sum(arms * arms, axis=1, keepdims=True),
            jnp.ones((2 * clumps, 1, spheres), jnp.float32),
            jnp.zeros((2 * clumps, 3, spheres), jnp.float32),
        ],
        axis=1,
    )
    batch = 4
    pulled = call(
        functools.partial(contact_kernel, clumps, batch),
        (clumps, 8, spheres),
        (contact_partner, centers),
        (near,),
        clumps,
    )
    carried = call(
        functools.partial(fluid_kernel, clumps, batch),
        (clumps, 8, spheres),
        (
            (margin_device * cells + margin_block).reshape(-1),
            (margin_offset - 0.5).reshape(-1),
        ),
        (near[:clumps], table),
        2 * clumps,
    )
    force = DRAG * (carried[:, 4:7] - clump_vel[:, :, None] * carried[:, 7:8]) + STIFF * (
        clump_arm * pulled[:, 3:4] - pulled[:, 0:3]
    )
    load = jnp.concatenate(
        [jnp.sum(force, axis=2), jnp.sum(jnp.cross(clump_arm, force, axis=1), axis=2)], axis=1
    )
    return (fluid_density, load.T)


def solution(mesh):
    in_specs = (
        P("stream", "span", None, None),
        P("stream", "span", None, None),
        P("stream", "span", None),
        P("stream", "span"),
        P(AXES, None),
        P(AXES, None),
        P(AXES, None, None),
        P(AXES, None),
        P(AXES, None),
        P(AXES, None, None),
        P(AXES),
    )
    out_specs = (P("stream", "span", None), P(None, AXES))
    return jax.shard_map(body, mesh=mesh, in_specs=in_specs, out_specs=out_specs, check_vma=False)
```

time: 717 us -> 240 us (0.33)
  other arithmetic: 334 us -> 13.8 us
  matrix products: 208 us -> 0 us
  Pallas kernels: 0 us -> 158 us
  local copies, waits for them, and re-layouts: 126 us -> 14.7 us
  starting transfers between devices: 38.3 us -> 16.6 us
  waiting for transfers between devices: 5.02 us -> 21.8 us
  between operations: 1.26 us -> 14.3 us
    reduce_sum x63 -> x3, other arithmetic: 295 us -> 6.57 us  [the longest x1 4.75 us: body(): jnp.sum(force, axis=2)]
    dot_general x21 -> x0, matrix products: 208 us -> none  [the longest x16 152 us: tile_force(): acc = jnp.dot(amp, kernel, precision=lax.Precision.HIGHEST)]
    pallas_call x0 -> x3, Pallas kernels: none -> 158 us  [call(): pl.pallas_call(kernel, out_shape=jax.ShapeDtypeStruct(shape, jnp.float32)...]
    gather x8 -> x0, local copies, waits for them, and re-layouts: 72.7 us -> none  [the longest x1 16.5 us: body(): clump_arm[source_clump] * keep[:, None, None]]
    all_to_all x4 -> x0, starting transfers between devices: 24 us -> none  [the longest x1 8.77 us: body(): lax.all_to_all(block_buf, ('stream', 'span'), split_axis=0, concat_axis=0...]
    ppermute x1 -> x2, waiting for transfers between devices: 0.01 us -> 19.7 us  [the longest x1 19.6 us: body(): arm_next = lax.ppermute(clump_arm, AXES, back)]
    add x18 -> x1, other arithmetic: 19.1 us -> 0.01 us  [body(): margin_device * cells + margin_block]
    sub x22 -> x1, local copies, waits for them, and re-layouts: 16.5 us -> 0.27 us  [body(): margin_offset - 0.5]
  transfers between devices with their start and end apart: 9 -> 7, of which waited for: 1 -> 3; matrix products, arithmetic and copies ran while one was open for 36% -> 5% of each run, Pallas kernels for 0% -> 29%
where the time goes in v1:
time: 240 us; the launch traced here: 239 us
  Pallas kernels  158 us (66%)
  waiting for transfers between devices  21.8 us (9%)
  starting transfers between devices  16.6 us (7%)
  local copies, waits for them, and re-layouts  14.7 us (6%)
  between operations  14.3 us (6%)
  other arithmetic  13.8 us (6%)
    pallas_call x3, Pallas kernels, call(): pl.pallas_call(kernel, out_shape=jax.ShapeDtypeStruct(shape, jnp.float32)...  158 us
    ppermute x1, waiting for transfers between devices, body(): arm_next = lax.ppermute(clump_arm, AXES, back)  19.6 us
    ppermute x2, starting transfers between devices, extended(): lax.ppermute(tail, axis, [(i, (i + 1) % count) for i in range(ends)])  8.59 us
    ppermute x1, starting transfers between devices, body(): center_next = lax.ppermute(clump_center, AXES, back)  5.22 us
  transfers between devices with their start and end apart: 7, of which 3 were waited for; matrix products, arithmetic and copies ran while one was open for 5% of the time, Pallas kernels for 29%

profile of v1, /device:TPU:0, one launch (start us, length us, event | category | flops | bytes accessed | tf_op | source)
XLA Modules:
  0.0 239.0 jit_solution(13899392519541281547)
XLA Ops:
  7.2 0.0 all-gather.2.cloned.1.call-start
  7.2 0.9 copy_add_fusion
  8.1 0.8 fusion.5
  9.0 1.3 collective-permute-start.1
  10.3 3.0 %collective-permute-start = (f32[1,8,4,128]{3,2,1,0:T(4,128)S(1)}, f32[1,8,4,128]{3,2,1,0:T(4,128)S(1)}, u32[]{:S(2)}, u32[]{:S(2)}) collective-permute-start(f32[1,8,4,128]{3,2,1,0:T(4,128)S(1)} %get-tuple-element.17), channel_id=1, source_target_pairs={{0,4},{4,8},{8,12},{12,16},{16,20},{20,24},{24,28},{1,5},{5,9},{9,... | collective-permute-start | bytes 49160 | tf_op jit(solution)/shard_map/ppermute | solution.py:27
  13.4 0.8 collective-permute-done
  14.2 1.3 collective-permute-start.3
  15.5 5.6 %collective-permute-start.2 = (f32[10,1,4,128]{3,2,1,0:T(4,128)S(1)}, f32[10,1,4,128]{3,2,1,0:T(4,128)S(1)}, u32[]{:S(2)}, u32[]{:S(2)}) collective-permute-start(f32[10,1,4,128]{3,2,1,0:T(4,128)S(1)} %get-tuple-element.15), channel_id=1, source_target_pairs={{0,1},{1,2},{2,3},{4,5},{5,6},{6,7},{8,9},{9,10},{10,11},{12,13},{... | collective-permute-start | bytes 61448 | tf_op jit(solution)/shard_map/ppermute | solution.py:27
  21.1 0.1 pad.17.clone
  21.1 0.1 pad.8.clone
  21.2 1.3 collective-permute-done.2
  22.5 0.2 compare_select_fusion
  22.7 0.1 pad_maximum_fusion.1
  22.8 0.9 maximum_maximum_fusion.1.cells_ref
  23.7 26.7 %shard_map.122 = f32[64,128]{1,0:T(8,128)} custom-call(f32[10,10,8,128]{3,2,1,0:T(8,128)} %maximum_maximum_fusion.1.cells_ref), custom_call_target="tpu_custom_call" | custom-call | flops 1207959552 | bytes 409600 | tf_op jit(solution)/shard_map/pallas_call | solution.py:162
  50.4 1.4 fusion.8
  51.8 0.8 pad_maximum_fusion
  52.6 0.0 all-gather.2.cloned.1.call-update
  52.7 5.2 %collective-permute-start.5 = (f32[512,3]{0,1:T(4,128)S(1)}, f32[512,3]{0,1:T(4,128)S(1)}, u32[]{:S(2)}, u32[]{:S(2)}) collective-permute-start(f32[512,3]{0,1:T(4,128)S(1)} %copy-done.9), channel_id=1, source_target_pairs={{0,31},{1,0},{2,1},{3,2},{4,3},{5,4},{6,5},{7,6},{8,7},{9,8},{10,9... | collective-permute-start | bytes 18440 | tf_op jit(solution)/shard_map/ppermute | solution.py:222
  57.9 0.2 collective-permute-start.4
  58.1 0.5 copy_dynamic-update-slice_fusion
  58.7 0.1 pad.14.clone
  58.8 0.1 pad.13.clone
  58.8 0.2 copy.71
  59.0 0.8 reshape.146.block_ref
  59.7 0.3 copy.72
  60.0 1.2 reshape.147.offset_ref
  61.2 0.9 copy.77
  62.1 0.2 copy.78
  62.3 0.9 reshape.148.center_ref
  63.2 19.6 %collective-permute-done.4 = f32[512,3,128]{2,0,1:T(8,128)} collective-permute-done((f32[512,3,128]{2,0,1:T(8,128)S(1)}, f32[512,3,128]{2,0,1:T(8,128)}, u32[]{:S(2)}, u32[]{:S(2)}) %collective-permute-start.4) | collective-permute-done | bytes 786464 | tf_op jit(solution)/shard_map/ppermute | solution.py:223
  82.9 1.7 copy_dynamic-update-slice_fusion.1
  84.6 1.5 multiply_reduce_fusion
  86.2 1.0 maximum_maximum_fusion.near_ref
  87.2 2.0 copy-done
  89.1 1.4 slice.75.near_ref
  90.6 69.8 %shard_map.124 = f32[512,8,128]{2,1,0:T(8,128)} custom-call(s32[512]{0:T(512)} %partner_ref.1, f32[3072]{0:T(1024)} %reshape.148.center_ref, f32[1024,8,128]{2,1,0:T(8,128)} %copy-done), custom_call_target="tpu_custom_call" | custom-call | flops 1073741824 | bytes 4194304 | tf_op jit(solution)/shard_map/pallas_call | solution.py:162
  160.4 1.8 slice.78
  162.2 0.0 all-gather.2.cloned.1.call-done.table_ref
  162.3 61.3 %shard_map.123 = f32[512,8,128]{2,1,0:T(8,128)} custom-call(s32[1024]{0:T(1024)} %reshape.146.block_ref, f32[3072]{0:T(1024)} %reshape.147.offset_ref, f32[512,8,128]{2,1,0:T(8,128)} %slice.75.near_ref, f32[2048,8,128]{2,1,0:T(8,128)} %all-gather.2.cloned.1.call-done.table_ref), custom_call_target="tpu_custom_call" | custom-call | flops 2147483648 | bytes 10485760 | tf_op jit(solution)/shard_map/pallas_call | solution.py:162
  223.5 1.8 slice.77
  225.4 4.7 %fusion.6 = (f32[512,3]{1,0:T(8,128)S(1)}, f32[512,3,128]{2,1,0:T(4,128)S(1)}) fusion(f32[512,8,128]{2,1,0:T(8,128)S(1)} %copy-done.3, f32[512,128]{1,0:T(8,128)S(1)} %bitcast.37, f32[512,3,128]{2,0,1:T(8,128)S(1)} %copy-done.1, f32[512,128]{1,0:T(8,128)S(1)} %bitcast.38, f32[512,3]{1,0:T(8,128)S(1)} %copy-done.2, f32[512,8,128]{2,1,0:T(8,128)} %shard_map.123), kind=kLoop, calls=%fused_computation.36 | loop fusion | flops 1571328 | bytes 3682304 | tf_op jit(solution)/shard_map/reduce_sum | solution.py:257
  230.1 0.5 fusion.10
  230.7 0.1 copy.85
  230.8 0.1 subtract_bitcast_fusion.1
  230.9 0.4 multiply_subtract_fusion
  231.3 0.3 maximum_reduce_fusion
  231.6 0.6 maximum_bitcast_fusion
  (35 shorter events, 0.2 us)
Async XLA Ops:
  7.2 155.1 %all-gather.2.cloned.1.call-start = ((), (), s32[]{:S(2)}) async-start(), calls=%async_computation | async-start | bytes 8650752 | tf_op jit(solution)/shard_map/all_gather | solution.py:220
  9.0 4.3 %collective-permute-start.1 = (f32[1,8,4,128]{3,2,1,0:T(4,128)S(1)}, f32[1,8,4,128]{3,2,1,0:T(4,128)S(1)}, u32[]{:S(2)}, u32[]{:S(2)}) collective-permute-start(f32[1,8,4,128]{3,2,1,0:T(4,128)S(1)} %get-tuple-element.18), channel_id=1, source_target_pairs={{4,0},{8,4},{12,8},{16,12},{20,16},{24,20},{28,24},{5,1},{9,5},{13... | collective-permute-start | bytes 49160 | tf_op jit(solution)/shard_map/ppermute | solution.py:29
  10.3 3.9 %collective-permute-start = (f32[1,8,4,128]{3,2,1,0:T(4,128)S(1)}, f32[1,8,4,128]{3,2,1,0:T(4,128)S(1)}, u32[]{:S(2)}, u32[]{:S(2)}) collective-permute-start(f32[1,8,4,128]{3,2,1,0:T(4,128)S(1)} %get-tuple-element.17), channel_id=1, source_target_pairs={{0,4},{4,8},{8,12},{12,16},{16,20},{20,24},{24,28},{1,5},{5,9},{9,... | collective-permute-start | bytes 49160 | tf_op jit(solution)/shard_map/ppermute | solution.py:27
  14.2 7.0 %collective-permute-start.3 = (f32[10,1,4,128]{3,2,1,0:T(4,128)S(1)}, f32[10,1,4,128]{3,2,1,0:T(4,128)S(1)}, u32[]{:S(2)}, u32[]{:S(2)}) collective-permute-start(f32[10,1,4,128]{3,2,1,0:T(4,128)S(1)} %get-tuple-element.16), channel_id=1, source_target_pairs={{1,0},{2,1},{3,2},{5,4},{6,5},{7,6},{9,8},{10,9},{11,10},{13,12},{... | collective-permute-start | bytes 61448 | tf_op jit(solution)/shard_map/ppermute | solution.py:29
  15.5 7.0 %collective-permute-start.2 = (f32[10,1,4,128]{3,2,1,0:T(4,128)S(1)}, f32[10,1,4,128]{3,2,1,0:T(4,128)S(1)}, u32[]{:S(2)}, u32[]{:S(2)}) collective-permute-start(f32[10,1,4,128]{3,2,1,0:T(4,128)S(1)} %get-tuple-element.15), channel_id=1, source_target_pairs={{0,1},{1,2},{2,3},{4,5},{5,6},{6,7},{8,9},{9,10},{10,11},{12,13},{... | collective-permute-start | bytes 61448 | tf_op jit(solution)/shard_map/ppermute | solution.py:27
  23.6 26.7 %copy-start.4 = (f32[8,8,128]{2,1,0:T(8,128)S(1)}, f32[8,8,128]{2,1,0:T(8,128)}, u32[]{:S(2)}) copy-start(f32[8,8,128]{2,1,0:T(8,128)} %param.13) | copy-start | bytes 98308
  23.6 26.7 %copy-start.6 = (s32[8,8]{1,0:T(8,128)S(1)}, s32[8,8]{1,0:T(8,128)}, u32[]{:S(2)}) copy-start(s32[8,8]{1,0:T(8,128)} %param.14) | copy-start | bytes 772
  23.6 28.1 %copy-start.5 = (f32[8,8,3,128]{3,1,2,0:T(8,128)S(1)}, f32[8,8,3,128]{3,1,2,0:T(8,128)}, u32[]{:S(2)}) copy-start(f32[8,8,3,128]{3,1,2,0:T(8,128)} %param.12) | copy-start | bytes 294916
  23.6 29.0 %copy-start.9 = (f32[512,3]{0,1:T(4,128)S(1)}, f32[512,3]{0,1:T(4,128)}, u32[]{:S(2)}) copy-start(f32[512,3]{0,1:T(4,128)} %param.15) | copy-start | bytes 18436
  23.6 34.3 %copy-start.1 = (f32[512,3,128]{2,0,1:T(8,128)S(1)}, f32[512,3,128]{2,0,1:T(8,128)}, u32[]{:S(2)}) copy-start(f32[512,3,128]{2,0,1:T(8,128)} %param.17) | copy-start | bytes 2359300
  23.6 34.4 %copy-start.7 = (f32[512,2,3]{0,1,2:T(2,128)S(1)}, f32[512,2,3]{0,1,2:T(2,128)}, u32[]{:S(2)}) copy-start(f32[512,2,3]{0,1,2:T(2,128)} %param.20) | copy-start | bytes 36868
  50.3 8.3 %copy-start.10 = (s32[512,2]{0,1:T(2,128)S(1)}, s32[512,2]{0,1:T(2,128)}, u32[]{:S(2)}) copy-start(s32[512,2]{0,1:T(2,128)} %param.19) | copy-start | bytes 12292
  50.3 8.3 %copy-start.11 = (s32[512,2]{0,1:T(2,128)S(1)}, s32[512,2]{0,1:T(2,128)}, u32[]{:S(2)}) copy-start(s32[512,2]{0,1:T(2,128)} %param.18) | copy-start | bytes 12292
  51.8 9.4 %copy-start.8 = (f32[512,3]{0,1:T(4,128)S(1)}, f32[512,3]{0,1:T(4,128)}, u32[]{:S(2)}) copy-start(f32[512,3]{0,1:T(4,128)} %param.16) | copy-start | bytes 18436
  52.7 9.4 %collective-permute-start.5 = (f32[512,3]{0,1:T(4,128)S(1)}, f32[512,3]{0,1:T(4,128)S(1)}, u32[]{:S(2)}, u32[]{:S(2)}) collective-permute-start(f32[512,3]{0,1:T(4,128)S(1)} %copy-done.9), channel_id=1, source_target_pairs={{0,31},{1,0},{2,1},{3,2},{4,3},{5,4},{6,5},{7,6},{8,7},{9,8},{10,9... | collective-permute-start | bytes 18440 | tf_op jit(solution)/shard_map/ppermute | solution.py:222
  57.9 25.0 %collective-permute-start.4 = (f32[512,3,128]{2,0,1:T(8,128)S(1)}, f32[512,3,128]{2,0,1:T(8,128)}, u32[]{:S(2)}, u32[]{:S(2)}) collective-permute-start(f32[512,3,128]{2,0,1:T(8,128)S(1)} %copy-done.1), channel_id=1, source_target_pairs={{0,31},{1,0},{2,1},{3,2},{4,3},{5,4},{6,5},{7,6},{8,7},{9,8},{10,9... | collective-permute-start | bytes 2359304 | tf_op jit(solution)/shard_map/ppermute | solution.py:223
  87.2 2.0 copy-start
  162.2 63.1 %copy-start.2 = (f32[512,3]{1,0:T(8,128)S(1)}, f32[512,3]{1,0:T(8,128)}, u32[]{:S(2)}) copy-start(f32[512,3]{1,0:T(8,128)} %copy.77) | copy-start | bytes 18436
  162.3 63.1 %copy-start.3 = (f32[512,8,128]{2,1,0:T(8,128)S(1)}, f32[512,8,128]{2,1,0:T(8,128)}, u32[]{:S(2)}) copy-start(f32[512,8,128]{2,1,0:T(8,128)} %shard_map.124) | copy-start | bytes 6291460
Sparse Core Ops, SparseCore 0:
  52.8 86.2 all-gather.1

commit v2 on v1

--- a/solution.py
+++ b/solution.py
@@ -42,7 +42,7 @@
 
 def near_stack(value):
     a, b, c = split(value)
-    return jnp.concatenate([a, a, a, b, b, c], axis=0).astype(jnp.bfloat16)
+    return turned(jnp.concatenate([a, a, a, b, b, c], axis=0))
 
 
 def far_stack(value):
@@ -66,10 +66,12 @@
     return jnp.where(row == 0, x, jnp.where(row == 1, y, jnp.where(row == 2, z, 0.0)))
 
 
+def turned(stack):
+    return stack.T.astype(jnp.bfloat16)
+
+
 def exponents(near, far):
-    return lax.dot_general(
-        near, far, (((0,), (0,)), ((), ())), preferred_element_type=jnp.float32
-    )
+    return jnp.dot(near, far, preferred_element_type=jnp.float32)
 
 
 def gathered_sum(amp, kernel):
@@ -86,20 +88,23 @@
 
 def density_kernel(rows_x, rows_y, cells_ref, out_ref):
     row = lax.broadcasted_iota(jnp.int32, (8, 128), 0)
+    steps = [(x, y) for x in (-1, 0, 1) for y in (-1, 0, 1)]
 
     def step(index, carry):
         bx = index // rows_y
         by = index % rows_y
         near = near_stack(near_rows(cells_ref[bx + 1, by + 1], row))
+        fars = []
+        for x, y in steps:
+            cell = cells_ref[bx + 1 + x, by + 1 + y]
+            point = jnp.where(row < 3, cell + column(row, float(x), float(y), 0.0), 0.0)
+            fars.append(far_stack(far_rows(point, row, INV_H, cell[3:4])))
         total = jnp.zeros((128, 128), jnp.float32)
-        for step_x in (-1, 0, 1):
-            for step_y in (-1, 0, 1):
-                cell = cells_ref[bx + 1 + step_x, by + 1 + step_y]
-                point = jnp.where(
-                    row < 3, cell + column(row, float(step_x), float(step_y), 0.0), 0.0
-                )
-                far = far_stack(far_rows(point, row, INV_H, cell[3:4]))
-                total = total + jnp.exp(exponents(near, far))
+        for k in range(0, len(fars), 2):
+            far = jnp.concatenate(fars[k : k + 2], axis=1)
+            kernel = jnp.exp(exponents(near, far))
+            for part in range(0, kernel.shape[1], 128):
+                total = total + kernel[:, part : part + 128]
         out_ref[pl.ds(index, 1), :] = jnp.sum(total.T, axis=0, keepdims=True)
         return carry
 
@@ -110,6 +115,7 @@
     row = lax.broadcasted_iota(jnp.int32, (8, 128), 0)
 
     def step(index, carry):
+        nears, points = [], []
         for k in range(batch):
             c = index * batch + k
             p = partner_ref[c]
@@ -119,58 +125,84 @@
                 center_ref[3 * p + 1] - center_ref[3 * c + 1],
                 center_ref[3 * p + 2] - center_ref[3 * c + 2],
             )
-            near = near_stack(near_ref[c])
-            point = jnp.where(row < 3, near_ref[p] + shift, 0.0)
-            far = far_stack(far_rows(point, row, INV_SIG, 0.0))
-            kernel = jnp.exp(exponents(near, far)).astype(jnp.bfloat16)
-            amp = amp_stack(jnp.where(row == 3, 1.0, point))
-            out_ref[c] = gathered_sum(amp, kernel)
+            nears.append(near_ref[c])
+            points.append(jnp.where(row < 3, near_ref[p] + shift, 0.0))
+        nears = [near_stack(near) for near in nears]
+        fars = [far_stack(far_rows(point, row, INV_SIG, 0.0)) for point in points]
+        amps = [amp_stack(jnp.where(row == 3, 1.0, point)) for point in points]
+        logs = [exponents(near, far) for near, far in zip(nears, fars)]
+        kernels = [jnp.exp(log).astype(jnp.bfloat16) for log in logs]
+        sums = [gathered_sum(amp, kernel) for amp, kernel in zip(amps, kernels)]
+        for k in range(batch):
+            out_ref[index * batch + k] = sums[k]
         return carry
 
     lax.fori_loop(0, clumps // batch, step, 0)
 
 
-def fluid_kernel(clumps, batch, block_ref, offset_ref, near_ref, table_ref, out_ref):
+def fluid_kernel(
+    clumps, batch, block_ref, offset_ref, near_ref, weight_ref, hbm_ref, out_ref, table_ref, sem
+):
     row = lax.broadcasted_iota(jnp.int32, (8, 128), 0)
+    filled = hbm_ref.shape[0]
+    fetch = pltpu.make_async_copy(hbm_ref, table_ref.at[pl.ds(0, filled)], sem)
+    fetch.start()
+    table_ref[filled:] = jnp.zeros((8, 128), jnp.float32)
+    fetch.wait()
 
     def step(index, carry):
+        nears, cells, weights, shifts = [], [], [], []
         for k in range(batch):
             c = index * batch + k
-            near = near_stack(near_ref[c])
-            fars, amps = [], []
+            nears.append(near_ref[c])
             for m in range(2):
                 e = 2 * c + m
-                cell = table_ref[block_ref[e]]
-                shift = column(
-                    row, offset_ref[3 * e], offset_ref[3 * e + 1], offset_ref[3 * e + 2]
+                block = block_ref[e]
+                cells.append(table_ref[pl.ds(6 * block, 8), :])
+                weights.append(weight_ref[pl.ds(block, 1), :])
+                shifts.append(
+                    column(row, offset_ref[3 * e], offset_ref[3 * e + 1], offset_ref[3 * e + 2])
                 )
-                point = jnp.where(row < 3, cell - shift, 0.0)
-                fars.append(far_stack(far_rows(point, row, INV_H, 0.0)))
-                amps.append(amp_stack(cell))
-            far = jnp.concatenate(fars, axis=1)
-            amp = jnp.concatenate(amps, axis=1)
-            kernel = jnp.exp(exponents(near, far)).astype(jnp.bfloat16)
-            out_ref[c] = gathered_sum(amp, kernel)
+        nears = [near_stack(near) for near in nears]
+        points = [jnp.where(row < 3, cell - shift, 0.0) for cell, shift in zip(cells, shifts)]
+        fars = [far_stack(far_rows(point, row, INV_H, 0.0)) for point in points]
+        amps = [
+            amp_stack(jnp.where(row == 6, 1.0, jnp.where(row == 7, 0.0, cell)) * weight)
+            for cell, weight in zip(cells, weights)
+        ]
+        logs = [
+            exponents(near, jnp.concatenate(fars[2 * k : 2 * k + 2], axis=1))
+            for k, near in enumerate(nears)
+        ]
+        kernels = [jnp.exp(log).astype(jnp.bfloat16) for log in logs]
+        sums = [
+            gathered_sum(jnp.concatenate(amps[2 * k : 2 * k + 2], axis=1), kernel)
+            for k, kernel in enumerate(kernels)
+        ]
+        for k in range(batch):
+            out_ref[index * batch + k] = sums[k]
         return carry
 
     lax.fori_loop(0, clumps // batch, step, 0)
 
 
-def call(kernel, shape, scalars, arrays, tiles):
+def call(kernel, shape, scalars, arrays, tiles, held=(), scratch=()):
     smem = pl.BlockSpec(memory_space=pltpu.SMEM)
     vmem = pl.BlockSpec(memory_space=pltpu.VMEM)
     return pl.pallas_call(
         kernel,
         out_shape=jax.ShapeDtypeStruct(shape, jnp.float32),
-        in_specs=[smem] * len(scalars) + [vmem] * len(arrays),
+        in_specs=[smem] * len(scalars) + [vmem] * len(arrays)
+        + [pl.BlockSpec(memory_space=pl.ANY)] * len(held),
         out_specs=vmem,
+        scratch_shapes=list(scratch),
         compiler_params=pltpu.CompilerParams(vmem_limit_bytes=VMEM_BYTES),
         cost_estimate=pl.CostEstimate(
-            flops=tiles * 128 * 128 * 128,
+            flops=tiles * 128 * 128 * 128 * 24,
             bytes_accessed=4 * sum(a.size for a in arrays),
             transcendentals=tiles * 128 * 128,
         ),
-    )(*scalars, *arrays)
+    )(*scalars, *arrays, *held)
 
 
 def body(
@@ -197,6 +229,8 @@
     live = (lanes[None, None, :] < fluid_count[..., None]).astype(jnp.float32)
     live_mass = live * fluid_mass
     centered = fluid_pos - 0.5
+    table = jnp.concatenate([centered, fluid_vel], axis=2).reshape(cells * 6, width)
+    table = lax.all_gather(table, AXES, axis=0, tiled=True)
     packed = jnp.concatenate([centered, live_mass[:, :, None, :]], axis=2)
     padded = extended(packed, (("stream", 0), ("span", 1)), 1)
     mass = padded[:, :, 3:4]
@@ -213,11 +247,9 @@
         9 * cells,
     )
     fluid_density = DENS * (fluid_mass + sums.reshape(rows_x, rows_y, width))
-    weight = (live_mass / fluid_density)[:, :, None, :]
-    table = jnp.concatenate(
-        [centered, jnp.zeros_like(weight), fluid_vel * weight, weight], axis=2
-    ).reshape(cells, 8, width)
-    table = lax.all_gather(table, AXES, axis=0, tiled=True)
+    weights = lax.all_gather(
+        (live_mass / fluid_density).reshape(cells, width), AXES, axis=0, tiled=True
+    )
 
     center_next = lax.ppermute(clump_center, AXES, back)
     arm_next = lax.ppermute(clump_arm, AXES, back)
@@ -247,10 +279,15 @@
             (margin_device * cells + margin_block).reshape(-1),
             (margin_offset - 0.5).reshape(-1),
         ),
-        (near[:clumps], table),
+        (near[:clumps], weights),
         2 * clumps,
-    )
-    force = DRAG * (carried[:, 4:7] - clump_vel[:, :, None] * carried[:, 7:8]) + STIFF * (
+        (table,),
+        (
+            pltpu.VMEM((table.shape[0] + 8, width), jnp.float32),
+            pltpu.SemaphoreType.DMA,
+        ),
+    )
+    force = DRAG * (carried[:, 3:6] - clump_vel[:, :, None] * carried[:, 6:7]) + STIFF * (
         clump_arm * pulled[:, 3:4] - pulled[:, 0:3]
     )
     load = jnp.concatenate(

time: 240 us -> 261 us (1.087)
  waiting for transfers between devices: 21.8 us -> 61.1 us
  Pallas kernels: 158 us -> 140 us
    all_gather x1, waiting for transfers between devices: 0.02 us -> 44.1 us  [body(): table = lax.all_gather(table, AXES, axis=0, tiled=True)]
    pallas_call x3, Pallas kernels: 158 us -> 140 us  [call(): pl.pallas_call(kernel, out_shape=jax.ShapeDtypeStruct(shape, jnp.float32)...]
    ppermute x1, waiting for transfers between devices: 19.6 us -> 14.7 us  [body(): arm_next = lax.ppermute(clump_arm, AXES, back)]
  transfers between devices with their start and end apart: 7 -> 8, of which waited for: 3 -> 4; matrix products, arithmetic and copies ran while one was open for 5% -> 5% of each run, Pallas kernels for 29% -> 21%
where the time goes in v2:
time: 261 us
  Pallas kernels  140 us (54%)
  waiting for transfers between devices  61.1 us (23%)
  starting transfers between devices  16.6 us (6%)
  local copies, waits for them, and re-layouts  15.4 us (6%)
  between operations  14.3 us (5%)
  other arithmetic  13.4 us (5%)
    pallas_call x3, Pallas kernels, call(): pl.pallas_call(kernel, out_shape=jax.ShapeDtypeStruct(shape, jnp.float32)...  140 us
    all_gather x1, waiting for transfers between devices, body(): table = lax.all_gather(table, AXES, axis=0, tiled=True)  44.1 us
    ppermute x1, waiting for transfers between devices, body(): arm_next = lax.ppermute(clump_arm, AXES, back)  14.7 us
    ppermute x2, starting transfers between devices, extended(): lax.ppermute(tail, axis, [(i, (i + 1) % count) for i in range(ends)])  8.59 us
  transfers between devices with their start and end apart: 8, of which 4 were waited for; matrix products, arithmetic and copies ran while one was open for 5% of the time, Pallas kernels for 21%

profile of v2, /device:TPU:0, one launch (start us, length us, event | category | flops | bytes accessed | tf_op | source)
XLA Modules:
  0.0 260.7 jit_solution(6737664894795893986)
XLA Ops:
  7.2 0.0 all-gather.3.cloned.1.call-start
  7.2 0.9 copy_add_fusion
  8.1 0.8 fusion.5
  9.0 1.3 collective-permute-start.1
  10.3 3.0 %collective-permute-start = (f32[1,8,4,128]{3,2,1,0:T(4,128)S(1)}, f32[1,8,4,128]{3,2,1,0:T(4,128)S(1)}, u32[]{:S(2)}, u32[]{:S(2)}) collective-permute-start(f32[1,8,4,128]{3,2,1,0:T(4,128)S(1)} %get-tuple-element.17), channel_id=1, source_target_pairs={{0,4},{4,8},{8,12},{12,16},{16,20},{20,24},{24,28},{1,5},{5,9},{9,... | collective-permute-start | bytes 49160 | tf_op jit(solution)/shard_map/ppermute | solution.py:27
  13.4 0.8 collective-permute-done
  14.2 1.3 collective-permute-start.3
  15.5 5.6 %collective-permute-start.2 = (f32[10,1,4,128]{3,2,1,0:T(4,128)S(1)}, f32[10,1,4,128]{3,2,1,0:T(4,128)S(1)}, u32[]{:S(2)}, u32[]{:S(2)}) collective-permute-start(f32[10,1,4,128]{3,2,1,0:T(4,128)S(1)} %get-tuple-element.15), channel_id=1, source_target_pairs={{0,1},{1,2},{2,3},{4,5},{5,6},{6,7},{8,9},{9,10},{10,11},{12,13},{... | collective-permute-start | bytes 61448 | tf_op jit(solution)/shard_map/ppermute | solution.py:27
  21.1 0.1 pad.15.clone
  21.1 1.4 collective-permute-done.2
  22.5 0.2 compare_select_fusion
  22.7 0.1 pad_maximum_fusion.1
  22.8 0.9 maximum_maximum_fusion.1.cells_ref
  23.7 27.0 %shard_map.122 = f32[64,128]{1,0:T(8,128)} custom-call(f32[10,10,8,128]{3,2,1,0:T(8,128)} %maximum_maximum_fusion.1.cells_ref), custom_call_target="tpu_custom_call" | custom-call | flops 28991029248 | bytes 409600 | tf_op jit(solution)/shard_map/pallas_call | solution.py:192
  50.7 1.5 divide_bitcast_fusion
  52.2 0.0 all-gather.5.cloned.1.call-start
  52.3 0.1 pad_maximum_fusion
  52.3 0.7 reshape.148
  53.1 5.2 %collective-permute-start.5 = (f32[512,3]{0,1:T(4,128)S(1)}, f32[512,3]{0,1:T(4,128)S(1)}, u32[]{:S(2)}, u32[]{:S(2)}) collective-permute-start(f32[512,3]{0,1:T(4,128)S(1)} %copy-done.8), channel_id=1, source_target_pairs={{0,31},{1,0},{2,1},{3,2},{4,3},{5,4},{6,5},{7,6},{8,7},{9,8},{10,9... | collective-permute-start | bytes 18440 | tf_op jit(solution)/shard_map/ppermute | solution.py:254
  58.3 0.2 collective-permute-start.4
  58.5 0.5 copy_dynamic-update-slice_fusion
  59.1 0.1 pad.12.clone
  59.1 0.1 pad.11.clone
  59.2 0.2 copy.69
  59.4 0.8 reshape.145.block_ref
  60.1 0.3 copy.70
  60.4 1.2 reshape.146.offset_ref
  61.6 0.8 copy.74
  62.5 0.2 copy.75
  62.7 0.9 reshape.149.center_ref
  63.6 14.7 %collective-permute-done.4 = f32[512,3,128]{2,0,1:T(8,128)} collective-permute-done((f32[512,3,128]{2,0,1:T(8,128)S(1)}, f32[512,3,128]{2,0,1:T(8,128)}, u32[]{:S(2)}, u32[]{:S(2)}) %collective-permute-start.4) | collective-permute-done | bytes 786464 | tf_op jit(solution)/shard_map/ppermute | solution.py:255
  78.3 1.7 copy_dynamic-update-slice_fusion.1
  80.1 1.5 multiply_reduce_fusion
  81.6 1.0 maximum_maximum_fusion.near_ref
  82.6 2.0 copy-done
  84.6 1.5 slice.75.near_ref
  86.1 55.0 %shard_map.124 = f32[512,8,128]{2,1,0:T(8,128)} custom-call(s32[512]{0:T(512)} %partner_ref.1, f32[3072]{0:T(1024)} %reshape.149.center_ref, f32[1024,8,128]{2,1,0:T(8,128)} %copy-done), custom_call_target="tpu_custom_call" | custom-call | flops 25769803776 | bytes 4194304 | tf_op jit(solution)/shard_map/pallas_call | solution.py:192
  141.1 1.8 slice.78
  143.0 44.1 %all-gather.5.cloned.1.call-done.hbm_ref = f32[12288,128]{1,0:T(8,128)} async-done(((f32[384,128]{1,0:T(8,128)}), f32[12288,128]{1,0:T(8,128)}) %all-gather.5.cloned.1.call-update) | async-done | bytes 6291472 | tf_op jit(solution)/shard_map/all_gather | solution.py:233
  187.1 57.7 %shard_map.123 = f32[512,8,128]{2,1,0:T(8,128)} custom-call(s32[1024]{0:T(1024)} %reshape.145.block_ref, f32[3072]{0:T(1024)} %reshape.146.offset_ref, f32[512,8,128]{2,1,0:T(8,128)} %slice.75.near_ref, f32[2048,128]{1,0:T(8,128)} %all-gather.3.cloned.1.call-done.weight_ref, f32[12288,128]{1,0:T(8,128)} %all-gather.5.cloned.1.call-done.hbm_ref), custom_call_target="tpu_custom_call" | custom-call | flops 51539607552 | bytes 3145728 | tf_op jit(solution)/shard_map/pallas_call | solution.py:192
  244.9 1.8 slice.77
  246.7 5.1 %fusion.6 = (f32[512,3]{1,0:T(8,128)S(1)}, f32[512,3,128]{2,1,0:T(4,128)S(1)}) fusion(f32[512,8,128]{2,1,0:T(8,128)} %shard_map.124, f32[512,128]{1,0:T(8,128)S(1)} %bitcast.32, f32[512,3,128]{2,0,1:T(8,128)S(1)} %copy-done.1, f32[512,128]{1,0:T(8,128)S(1)} %bitcast.33, f32[512,3]{1,0:T(8,128)S(1)} %copy-done.2, f32[512,8,128]{2,1,0:T(8,128)} %shard_map.123), kind=kLoop, calls=%fused_computation.36 | loop fusion | flops 1571328 | bytes 3682304 | tf_op jit(solution)/shard_map/reduce_sum | solution.py:294
  251.8 0.5 fusion.9
  252.3 0.1 copy.82
  252.4 0.1 subtract_bitcast_fusion.1
  252.5 0.4 multiply_subtract_fusion
  252.9 0.3 maximum_reduce_fusion
  253.2 0.6 maximum_bitcast_fusion
  (35 shorter events, 0.2 us)
Async XLA Ops:
  7.2 135.8 %all-gather.3.cloned.1.call-start = ((), (), s32[]{:S(2)}) async-start(), calls=%async_computation | async-start | bytes 1081344 | tf_op jit(solution)/shard_map/all_gather | solution.py:250
  9.0 4.3 %collective-permute-start.1 = (f32[1,8,4,128]{3,2,1,0:T(4,128)S(1)}, f32[1,8,4,128]{3,2,1,0:T(4,128)S(1)}, u32[]{:S(2)}, u32[]{:S(2)}) collective-permute-start(f32[1,8,4,128]{3,2,1,0:T(4,128)S(1)} %get-tuple-element.18), channel_id=1, source_target_pairs={{4,0},{8,4},{12,8},{16,12},{20,16},{24,20},{28,24},{5,1},{9,5},{13... | collective-permute-start | bytes 49160 | tf_op jit(solution)/shard_map/ppermute | solution.py:29
  10.3 3.9 %collective-permute-start = (f32[1,8,4,128]{3,2,1,0:T(4,128)S(1)}, f32[1,8,4,128]{3,2,1,0:T(4,128)S(1)}, u32[]{:S(2)}, u32[]{:S(2)}) collective-permute-start(f32[1,8,4,128]{3,2,1,0:T(4,128)S(1)} %get-tuple-element.17), channel_id=1, source_target_pairs={{0,4},{4,8},{8,12},{12,16},{16,20},{20,24},{24,28},{1,5},{5,9},{9,... | collective-permute-start | bytes 49160 | tf_op jit(solution)/shard_map/ppermute | solution.py:27
  14.2 7.0 %collective-permute-start.3 = (f32[10,1,4,128]{3,2,1,0:T(4,128)S(1)}, f32[10,1,4,128]{3,2,1,0:T(4,128)S(1)}, u32[]{:S(2)}, u32[]{:S(2)}) collective-permute-start(f32[10,1,4,128]{3,2,1,0:T(4,128)S(1)} %get-tuple-element.16), channel_id=1, source_target_pairs={{1,0},{2,1},{3,2},{5,4},{6,5},{7,6},{9,8},{10,9},{11,10},{13,12},{... | collective-permute-start | bytes 61448 | tf_op jit(solution)/shard_map/ppermute | solution.py:29
  15.5 7.0 %collective-permute-start.2 = (f32[10,1,4,128]{3,2,1,0:T(4,128)S(1)}, f32[10,1,4,128]{3,2,1,0:T(4,128)S(1)}, u32[]{:S(2)}, u32[]{:S(2)}) collective-permute-start(f32[10,1,4,128]{3,2,1,0:T(4,128)S(1)} %get-tuple-element.15), channel_id=1, source_target_pairs={{0,1},{1,2},{2,3},{4,5},{5,6},{6,7},{8,9},{9,10},{10,11},{12,13},{... | collective-permute-start | bytes 61448 | tf_op jit(solution)/shard_map/ppermute | solution.py:27
  23.6 27.0 %copy-start.3 = (f32[8,8,128]{2,1,0:T(8,128)S(1)}, f32[8,8,128]{2,1,0:T(8,128)}, u32[]{:S(2)}) copy-start(f32[8,8,128]{2,1,0:T(8,128)} %param.13) | copy-start | bytes 98308
  23.6 27.0 %copy-start.5 = (s32[8,8]{1,0:T(8,128)S(1)}, s32[8,8]{1,0:T(8,128)}, u32[]{:S(2)}) copy-start(s32[8,8]{1,0:T(8,128)} %param.14) | copy-start | bytes 772
  23.6 28.6 %copy-start.4 = (f32[8,8,3,128]{3,1,2,0:T(8,128)S(1)}, f32[8,8,3,128]{3,1,2,0:T(8,128)}, u32[]{:S(2)}) copy-start(f32[8,8,3,128]{3,1,2,0:T(8,128)} %param.12) | copy-start | bytes 294916
  23.6 29.4 %copy-start.8 = (f32[512,3]{0,1:T(4,128)S(1)}, f32[512,3]{0,1:T(4,128)}, u32[]{:S(2)}) copy-start(f32[512,3]{0,1:T(4,128)} %param.15) | copy-start | bytes 18436
  23.6 34.7 %copy-start.1 = (f32[512,3,128]{2,0,1:T(8,128)S(1)}, f32[512,3,128]{2,0,1:T(8,128)}, u32[]{:S(2)}) copy-start(f32[512,3,128]{2,0,1:T(8,128)} %param.17) | copy-start | bytes 2359300
  23.6 34.8 %copy-start.6 = (f32[512,2,3]{0,1,2:T(2,128)S(1)}, f32[512,2,3]{0,1,2:T(2,128)}, u32[]{:S(2)}) copy-start(f32[512,2,3]{0,1,2:T(2,128)} %param.20) | copy-start | bytes 36868
  50.7 8.3 %copy-start.9 = (s32[512,2]{0,1:T(2,128)S(1)}, s32[512,2]{0,1:T(2,128)}, u32[]{:S(2)}) copy-start(s32[512,2]{0,1:T(2,128)} %param.19) | copy-start | bytes 12292
  50.7 8.4 %copy-start.10 = (s32[512,2]{0,1:T(2,128)S(1)}, s32[512,2]{0,1:T(2,128)}, u32[]{:S(2)}) copy-start(s32[512,2]{0,1:T(2,128)} %param.18) | copy-start | bytes 12292
  52.2 135.0 %all-gather.5.cloned.1.call-start = ((), (), s32[]{:S(2)}) async-start(), calls=%async_computation.1 | async-start | bytes 6488064 | tf_op jit(solution)/shard_map/all_gather | solution.py:233
  52.3 9.3 %copy-start.7 = (f32[512,3]{0,1:T(4,128)S(1)}, f32[512,3]{0,1:T(4,128)}, u32[]{:S(2)}) copy-start(f32[512,3]{0,1:T(4,128)} %param.16) | copy-start | bytes 18436
  53.1 9.4 %collective-permute-start.5 = (f32[512,3]{0,1:T(4,128)S(1)}, f32[512,3]{0,1:T(4,128)S(1)}, u32[]{:S(2)}, u32[]{:S(2)}) collective-permute-start(f32[512,3]{0,1:T(4,128)S(1)} %copy-done.8), channel_id=1, source_target_pairs={{0,31},{1,0},{2,1},{3,2},{4,3},{5,4},{6,5},{7,6},{8,7},{9,8},{10,9... | collective-permute-start | bytes 18440 | tf_op jit(solution)/shard_map/ppermute | solution.py:254
  58.3 20.0 %collective-permute-start.4 = (f32[512,3,128]{2,0,1:T(8,128)S(1)}, f32[512,3,128]{2,0,1:T(8,128)}, u32[]{:S(2)}, u32[]{:S(2)}) collective-permute-start(f32[512,3,128]{2,0,1:T(8,128)S(1)} %copy-done.1), channel_id=1, source_target_pairs={{0,31},{1,0},{2,1},{3,2},{4,3},{5,4},{6,5},{7,6},{8,7},{9,8},{10,9... | collective-permute-start | bytes 2359304 | tf_op jit(solution)/shard_map/ppermute | solution.py:255
  82.6 2.0 copy-start
  142.9 103.7 %copy-start.2 = (f32[512,3]{1,0:T(8,128)S(1)}, f32[512,3]{1,0:T(8,128)}, u32[]{:S(2)}) copy-start(f32[512,3]{1,0:T(8,128)} %copy.74) | copy-start | bytes 18436
Sparse Core Ops, SparseCore 0:
  52.3 62.8 all-gather.2
  118.0 69.0 all-gather.4

commit v3 on v2

--- a/solution.py
+++ b/solution.py
@@ -33,41 +33,43 @@
     return cells
 
 
-def split(value):
-    high = value.astype(jnp.bfloat16).astype(jnp.float32)
-    rest = value - high
-    mid = rest.astype(jnp.bfloat16).astype(jnp.float32)
-    return high, mid, rest - mid
-
-
-def near_stack(value):
-    a, b, c = split(value)
-    return turned(jnp.concatenate([a, a, a, b, b, c], axis=0))
-
-
-def far_stack(value):
-    a, b, c = split(value)
-    return jnp.concatenate([a, b, c, a, b, a], axis=0).astype(jnp.bfloat16)
-
-
-def near_rows(point, row):
-    point = jnp.where(row < 3, point, 0.0)
-    norm = jnp.sum(point * point, axis=0, keepdims=True)
-    return jnp.where(row == 3, norm, jnp.where(row == 4, 1.0, point))
-
-
-def far_rows(point, row, scale, extra):
-    norm = jnp.sum(point * point, axis=0, keepdims=True)
-    last = extra - scale * norm
-    return jnp.where(row == 3, -scale, jnp.where(row == 4, last, (2.0 * scale) * point))
+def rounded(value):
+    return value.astype(jnp.bfloat16).astype(jnp.float32)
+
+
+def near_stack(point, row):
+    point = jnp.where(row < 3, point, jnp.where(row == 3, 1.0, 0.0))
+    high = rounded(point)
+    low = jnp.where(row == 3, 1.0, point - high)
+    return [high + pltpu.roll(high, 4, 0), low]
+
+
+def far_stack(point, row, scale, extra):
+    last = extra - scale * jnp.sum(point * point, axis=0, keepdims=True)
+    value = jnp.where(row == 3, last, (2.0 * scale) * point)
+    high = rounded(value)
+    mid = rounded(value - high)
+    third = jnp.where(row == 3, value - high - mid, high)
+    return jnp.concatenate([high + pltpu.roll(mid, 4, 0), third], axis=0).astype(jnp.bfloat16)
+
+
+def placed(fars, at, count):
+    far = fars[0] if len(fars) == 1 else jnp.concatenate(fars, axis=1)
+    width = far.shape[1]
+    parts = [far]
+    if at:
+        parts = [jnp.zeros((16 * at, width), jnp.bfloat16)] + parts
+    if at < count - 1:
+        parts = parts + [jnp.zeros((16 * (count - 1 - at), width), jnp.bfloat16)]
+    return jnp.concatenate(parts, axis=0)
+
+
+def turned(stacks):
+    return jnp.concatenate(stacks, axis=0).T.astype(jnp.bfloat16)
 
 
 def column(row, x, y, z):
     return jnp.where(row == 0, x, jnp.where(row == 1, y, jnp.where(row == 2, z, 0.0)))
-
-
-def turned(stack):
-    return stack.T.astype(jnp.bfloat16)
 
 
 def exponents(near, far):
@@ -86,29 +88,38 @@
     return jnp.concatenate([high, value - high], axis=0).astype(jnp.bfloat16)
 
 
-def density_kernel(rows_x, rows_y, cells_ref, out_ref):
+def density_kernel(rows_x, rows_y, batch, cells_ref, out_ref):
     row = lax.broadcasted_iota(jnp.int32, (8, 128), 0)
     steps = [(x, y) for x in (-1, 0, 1) for y in (-1, 0, 1)]
 
     def step(index, carry):
-        bx = index // rows_y
-        by = index % rows_y
-        near = near_stack(near_rows(cells_ref[bx + 1, by + 1], row))
-        fars = []
-        for x, y in steps:
-            cell = cells_ref[bx + 1 + x, by + 1 + y]
-            point = jnp.where(row < 3, cell + column(row, float(x), float(y), 0.0), 0.0)
-            fars.append(far_stack(far_rows(point, row, INV_H, cell[3:4])))
-        total = jnp.zeros((128, 128), jnp.float32)
-        for k in range(0, len(fars), 2):
-            far = jnp.concatenate(fars[k : k + 2], axis=1)
-            kernel = jnp.exp(exponents(near, far))
-            for part in range(0, kernel.shape[1], 128):
-                total = total + kernel[:, part : part + 128]
-        out_ref[pl.ds(index, 1), :] = jnp.sum(total.T, axis=0, keepdims=True)
+        cells, norms, stacks = [], [], []
+        for k in range(batch):
+            cell = index * batch + k
+            cells.append((cell // rows_y, cell % rows_y))
+            center = cells_ref[cells[k][0] + 1, cells[k][1] + 1]
+            stacks += near_stack(center, row)
+            norms.append(jnp.sum(jnp.where(row < 3, center * center, 0.0), axis=0, keepdims=True))
+        near = turned(stacks)
+        sums = []
+        for k, (bx, by) in enumerate(cells):
+            fars = []
+            for x, y in steps:
+                cell = cells_ref[bx + 1 + x, by + 1 + y]
+                point = jnp.where(row < 3, cell + column(row, float(x), float(y), 0.0), 0.0)
+                fars.append(far_stack(point, row, INV_H, cell[3:4]))
+            total = None
+            for first in range(0, len(fars), 2):
+                kernel = jnp.exp(exponents(near, placed(fars[first : first + 2], k, batch)))
+                for part in range(0, kernel.shape[1], 128):
+                    piece = kernel[:, part : part + 128]
+                    total = piece if total is None else total + piece
+            sums.append(jnp.sum(total.T, axis=0, keepdims=True) * jnp.exp(-INV_H * norms[k]))
+        for k in range(batch):
+            out_ref[pl.ds(index * batch + k, 1), :] = sums[k]
         return carry
 
-    lax.fori_loop(0, rows_x * rows_y, step, 0)
+    lax.fori_loop(0, rows_x * rows_y // batch, step, 0)
 
 
 def contact_kernel(clumps, batch, partner_ref, center_ref, near_ref, out_ref):
@@ -127,12 +138,14 @@
             )
             nears.append(near_ref[c])
             points.append(jnp.where(row < 3, near_ref[p] + shift, 0.0))
-        nears = [near_stack(near) for near in nears]
-        fars = [far_stack(far_rows(point, row, INV_SIG, 0.0)) for point in points]
+        turn = turned([part for near in nears for part in near_stack(near, row)])
+        fars = [far_stack(point, row, INV_SIG, 0.0) for point in points]
         amps = [amp_stack(jnp.where(row == 3, 1.0, point)) for point in points]
-        logs = [exponents(near, far) for near, far in zip(nears, fars)]
-        kernels = [jnp.exp(log).astype(jnp.bfloat16) for log in logs]
-        sums = [gathered_sum(amp, kernel) for amp, kernel in zip(amps, kernels)]
+        sums = []
+        for k in range(batch):
+            log = exponents(turn, placed(fars[k : k + 1], k, batch))
+            total = gathered_sum(amps[k], jnp.exp(log).astype(jnp.bfloat16))
+            sums.append(total * jnp.exp(-INV_SIG * nears[k][3:4]))
         for k in range(batch):
             out_ref[index * batch + k] = sums[k]
         return carry
@@ -163,22 +176,19 @@
                 shifts.append(
                     column(row, offset_ref[3 * e], offset_ref[3 * e + 1], offset_ref[3 * e + 2])
                 )
-        nears = [near_stack(near) for near in nears]
+        turn = turned([part for near in nears for part in near_stack(near, row)])
         points = [jnp.where(row < 3, cell - shift, 0.0) for cell, shift in zip(cells, shifts)]
-        fars = [far_stack(far_rows(point, row, INV_H, 0.0)) for point in points]
+        fars = [far_stack(point, row, INV_H, 0.0) for point in points]
         amps = [
             amp_stack(jnp.where(row == 6, 1.0, jnp.where(row == 7, 0.0, cell)) * weight)
             for cell, weight in zip(cells, weights)
         ]
-        logs = [
-            exponents(near, jnp.concatenate(fars[2 * k : 2 * k + 2], axis=1))
-            for k, near in enumerate(nears)
-        ]
-        kernels = [jnp.exp(log).astype(jnp.bfloat16) for log in logs]
-        sums = [
-            gathered_sum(jnp.concatenate(amps[2 * k : 2 * k + 2], axis=1), kernel)
-            for k, kernel in enumerate(kernels)
-        ]
+        sums = []
+        for k in range(batch):
+            log = exponents(turn, placed(fars[2 * k : 2 * k + 2], k, batch))
+            amp = jnp.concatenate(amps[2 * k : 2 * k + 2], axis=1)
+            total = gathered_sum(amp, jnp.exp(log).astype(jnp.bfloat16))
+            sums.append(total * jnp.exp(-INV_H * nears[k][3:4]))
         for k in range(batch):
             out_ref[index * batch + k] = sums[k]
         return carry
@@ -198,9 +208,9 @@
         scratch_shapes=list(scratch),
         compiler_params=pltpu.CompilerParams(vmem_limit_bytes=VMEM_BYTES),
         cost_estimate=pl.CostEstimate(
-            flops=tiles * 128 * 128 * 128 * 24,
-            bytes_accessed=4 * sum(a.size for a in arrays),
-            transcendentals=tiles * 128 * 128,
+            flops=tiles * 128,
+            bytes_accessed=128 * tiles,
+            transcendentals=tiles * 128,
         ),
     )(*scalars, *arrays, *held)
 
@@ -240,16 +250,17 @@
         axis=2,
     )
     sums = call(
-        functools.partial(density_kernel, rows_x, rows_y),
+        functools.partial(density_kernel, rows_x, rows_y, 4),
         (cells, width),
         (),
         (padded,),
         9 * cells,
     )
     fluid_density = DENS * (fluid_mass + sums.reshape(rows_x, rows_y, width))
-    weights = lax.all_gather(
-        (live_mass / fluid_density).reshape(cells, width), AXES, axis=0, tiled=True
-    )
+    weights = (live_mass / fluid_density).reshape(cells, width)
+    weights, table = lax.optimization_barrier((weights, table))
+    weights = lax.all_gather(weights, "span", axis=0, tiled=True)
+    weights = lax.all_gather(weights, "stream", axis=0, tiled=True)
 
     center_next = lax.ppermute(clump_center, AXES, back)
     arm_next = lax.ppermute(clump_arm, AXES, back)
@@ -264,7 +275,7 @@
         ],
         axis=1,
     )
-    batch = 4
+    batch = 8
     pulled = call(
         functools.partial(contact_kernel, clumps, batch),
         (clumps, 8, spheres),

time: 261 us -> 252 us (0.966)
  Pallas kernels: 140 us -> 116 us
  blocking collectives: 0 us -> 14.1 us
  starting transfers between devices: 16.6 us -> 11.4 us
  other arithmetic: 13.4 us -> 16.9 us
    pallas_call x3, Pallas kernels: 140 us -> 116 us  [call(): pl.pallas_call(kernel, out_shape=jax.ShapeDtypeStruct(shape, jnp.float32)...]
    all_gather x0 -> x1, blocking collectives: none -> 14.1 us  [body(): weights = lax.all_gather(weights, 'span', axis=0, tiled=True)]
    ppermute x1, starting transfers between devices: 5.22 us -> 0.06 us  [body(): center_next = lax.ppermute(clump_center, AXES, back)]
  transfers between devices with their start and end apart: 8 -> 8, of which waited for: 4 -> 4; matrix products, arithmetic and copies ran while one was open for 5% -> 7% of each run, Pallas kernels for 21% -> 29%
where the time goes in v3:
time: 252 us; the launch traced here: 251 us
  Pallas kernels  116 us (46%)
  waiting for transfers between devices  61.5 us (24%)
  other arithmetic  16.9 us (7%)
  local copies, waits for them, and re-layouts  16.4 us (7%)
  between operations  14.4 us (6%)
  blocking collectives  14.1 us (6%)
  starting transfers between devices  11.4 us (5%)
    pallas_call x3, Pallas kernels, call(): pl.pallas_call(kernel, out_shape=jax.ShapeDtypeStruct(shape, jnp.float32)...  116 us
    all_gather x1, waiting for transfers between devices, body(): table = lax.all_gather(table, AXES, axis=0, tiled=True)  44.7 us
    ppermute x1, waiting for transfers between devices, body(): arm_next = lax.ppermute(clump_arm, AXES, back)  14.5 us
    all_gather x1, blocking collectives, body(): weights = lax.all_gather(weights, 'span', axis=0, tiled=True)  14.1 us
    ppermute x2, starting transfers between devices, extended(): lax.ppermute(tail, axis, [(i, (i + 1) % count) for i in range(ends)])  8.59 us
    reduce_sum x1, other arithmetic, body(): jnp.sum(force, axis=2)  5.41 us
  transfers between devices with their start and end apart: 8, of which 4 were waited for; matrix products, arithmetic and copies ran while one was open for 7% of the time, Pallas kernels for 29%

profile of v3, /device:TPU:0, one launch (start us, length us, event | category | flops | bytes accessed | tf_op | source)
XLA Modules:
  0.0 250.5 jit_solution(15728641514009831159)
XLA Ops:
  7.2 0.9 copy_add_fusion
  8.2 1.0 copy.73
  9.2 0.1 pad_maximum_fusion
  9.3 0.7 reshape.148
  10.1 0.8 fusion.5
  10.9 1.3 collective-permute-start.1
  12.2 3.0 %collective-permute-start = (f32[1,8,4,128]{3,2,1,0:T(4,128)S(1)}, f32[1,8,4,128]{3,2,1,0:T(4,128)S(1)}, u32[]{:S(2)}, u32[]{:S(2)}) collective-permute-start(f32[1,8,4,128]{3,2,1,0:T(4,128)S(1)} %get-tuple-element.21), channel_id=1, source_target_pairs={{0,4},{4,8},{8,12},{12,16},{16,20},{20,24},{24,28},{1,5},{5,9},{9,... | collective-permute-start | bytes 49160 | tf_op jit(solution)/shard_map/ppermute | solution.py:27
  15.3 0.8 collective-permute-done
  16.1 1.3 collective-permute-start.3
  17.4 5.6 %collective-permute-start.2 = (f32[10,1,4,128]{3,2,1,0:T(4,128)S(1)}, f32[10,1,4,128]{3,2,1,0:T(4,128)S(1)}, u32[]{:S(2)}, u32[]{:S(2)}) collective-permute-start(f32[10,1,4,128]{3,2,1,0:T(4,128)S(1)} %get-tuple-element.19), channel_id=1, source_target_pairs={{0,1},{1,2},{2,3},{4,5},{5,6},{6,7},{8,9},{9,10},{10,11},{12,13},{... | collective-permute-start | bytes 61448 | tf_op jit(solution)/shard_map/ppermute | solution.py:27
  23.0 0.1 pad.15.clone
  23.1 1.4 collective-permute-done.2
  24.5 0.2 compare_select_fusion
  24.6 0.1 pad_maximum_fusion.1
  24.7 0.9 maximum_maximum_fusion.1.cells_ref
  25.6 11.8 %shard_map.122 = f32[64,128]{1,0:T(8,128)} custom-call(f32[10,10,8,128]{3,2,1,0:T(8,128)} %maximum_maximum_fusion.1.cells_ref), custom_call_target="tpu_custom_call" | custom-call | flops 73728 | bytes 73728 | tf_op jit(solution)/shard_map/pallas_call | solution.py:202
  37.3 1.4 divide_bitcast_fusion
  38.7 44.7 %all-gather.3.cloned.1.call-done.hbm_ref = f32[12288,128]{1,0:T(8,128)} async-done(((f32[384,128]{1,0:T(8,128)}), f32[12288,128]{1,0:T(8,128)}) %all-gather.3.cloned.1.call-update) | async-done | bytes 6291472 | tf_op jit(solution)/shard_map/all_gather | solution.py:243
  83.4 14.1 %all_gather.10 = f32[256,128]{1,0:T(8,128)} all-gather(f32[64,128]{1,0:T(8,128)S(1)} %get-tuple-element.4), channel_id=1, replica_groups=mesh['stream'=8,'span'=4] {'span'}, dimensions={0}, use_global_device_ids=true | all-gather | bytes 163840 | tf_op jit(solution)/shard_map/all_gather | solution.py:262
  97.6 0.1 collective-permute-start.5
  97.7 0.1 collective-permute-start.4
  97.8 0.5 copy_dynamic-update-slice_fusion
  98.4 0.1 pad.12.clone
  98.4 0.1 pad.11.clone
  98.5 0.1 copy.69
  98.7 0.8 reshape.145.block_ref
  99.4 0.3 copy.70
  99.7 1.2 reshape.146.offset_ref
  100.9 0.8 copy.74
  101.8 0.2 copy.75
  102.0 0.9 reshape.149.center_ref
  102.9 14.5 %collective-permute-done.4 = f32[512,3,128]{2,0,1:T(8,128)} collective-permute-done((f32[512,3,128]{2,0,1:T(8,128)S(1)}, f32[512,3,128]{2,0,1:T(8,128)}, u32[]{:S(2)}, u32[]{:S(2)}) %collective-permute-start.4) | collective-permute-done | bytes 786464 | tf_op jit(solution)/shard_map/ppermute | solution.py:266
  117.3 1.7 copy_dynamic-update-slice_fusion.1
  119.1 1.5 multiply_reduce_fusion
  120.6 3.1 %maximum_maximum_fusion.near_ref = f32[1024,8,128]{2,1,0:T(8,128)} fusion(f32[1024,1,128]{2,1,0:T(1,128)S(1)} %bitcast.31, f32[1024,3,128]{2,1,0:T(4,128)S(1)} %copy_dynamic-update-slice_fusion.1, f32[8]{0:T(128)S(1)} %pad.12.clone, f32[8]{0:T(128)S(1)} %pad.11.clone), kind=kLoop, calls=%fused_computation | loop fusion | flops 3145728 | bytes 6291520 | tf_op jit(solution)/shard_map/concatenate | solution.py:269
  123.7 60.0 %shard_map.124 = f32[512,8,128]{2,1,0:T(8,128)} custom-call(s32[512]{0:T(512)} %partner_ref.1, f32[3072]{0:T(1024)} %reshape.149.center_ref, f32[1024,8,128]{2,1,0:T(8,128)} %maximum_maximum_fusion.near_ref), custom_call_target="tpu_custom_call" | custom-call | flops 65536 | bytes 65536 | tf_op jit(solution)/shard_map/pallas_call | solution.py:202
  183.7 1.5 slice.75.near_ref
  185.2 1.8 slice.78
  187.1 44.2 %shard_map.123 = f32[512,8,128]{2,1,0:T(8,128)} custom-call(s32[1024]{0:T(1024)} %reshape.145.block_ref, f32[3072]{0:T(1024)} %reshape.146.offset_ref, f32[512,8,128]{2,1,0:T(8,128)} %slice.75.near_ref, f32[2048,128]{1,0:T(8,128)} %all-gather.5.cloned.1.call-done.weight_ref, f32[12288,128]{1,0:T(8,128)} %all-gather.3.cloned.1.call-done.hbm_ref), custom_call_target="tpu_custom_call" | custom-call | flops 131072 | bytes 131072 | tf_op jit(solution)/shard_map/pallas_call | solution.py:202
  231.3 1.8 slice.77
  233.1 5.4 %fusion.6 = (f32[512,3]{1,0:T(8,128)}, f32[512,3,128]{2,1,0:T(4,128)S(1)}) fusion(f32[512,8,128]{2,1,0:T(8,128)S(1)} %copy-done.2, f32[512,128]{1,0:T(8,128)S(1)} %bitcast.32, f32[512,3,128]{2,0,1:T(8,128)S(1)} %copy-done.1, f32[512,128]{1,0:T(8,128)S(1)} %bitcast.33, f32[512,3]{1,0:T(8,128)S(1)} %copy-done.4, f32[512,8,128]{2,1,0:T(8,128)} %shard_map.123), kind=kLoop, calls=%fused_computation.36 | loop fusion | flops 1571328 | bytes 3682304 | tf_op jit(solution)/shard_map/reduce_sum | solution.py:305
  238.5 1.0 copy-done.3
  239.5 0.5 fusion.9
  240.0 1.1 copy.82
  241.1 0.1 subtract_bitcast_fusion.1
  241.2 1.6 multiply_subtract_fusion
  242.8 0.3 maximum_reduce_fusion
  243.1 0.6 maximum_bitcast_fusion
  (38 shorter events, 0.3 us)
Async XLA Ops:
  7.2 30.2 %copy-start.5 = (f32[8,8,128]{2,1,0:T(8,128)S(1)}, f32[8,8,128]{2,1,0:T(8,128)}, u32[]{:S(2)}) copy-start(f32[8,8,128]{2,1,0:T(8,128)} %param.13) | copy-start | bytes 98308
  7.2 30.1 %copy-start.6 = (s32[8,8]{1,0:T(8,128)S(1)}, s32[8,8]{1,0:T(8,128)}, u32[]{:S(2)}) copy-start(s32[8,8]{1,0:T(8,128)} %param.14) | copy-start | bytes 772
  7.2 76.3 %all-gather.3.cloned.1.call-start = ((), (), s32[]{:S(2)}) async-start(), calls=%async_computation | async-start | bytes 6488064 | tf_op jit(solution)/shard_map/all_gather | solution.py:243
  8.2 89.4 %copy-start.9 = (f32[512,3]{0,1:T(4,128)S(1)}, f32[512,3]{0,1:T(4,128)}, u32[]{:S(2)}) copy-start(f32[512,3]{0,1:T(4,128)} %param.15) | copy-start | bytes 18436
  8.2 89.5 %copy-start.1 = (f32[512,3,128]{2,0,1:T(8,128)S(1)}, f32[512,3,128]{2,0,1:T(8,128)}, u32[]{:S(2)}) copy-start(f32[512,3,128]{2,0,1:T(8,128)} %param.17) | copy-start | bytes 2359300
  8.2 89.5 %copy-start.7 = (f32[512,2,3]{0,1,2:T(2,128)S(1)}, f32[512,2,3]{0,1,2:T(2,128)}, u32[]{:S(2)}) copy-start(f32[512,2,3]{0,1,2:T(2,128)} %param.20) | copy-start | bytes 36868
  10.0 177.1 %all-gather.5.cloned.1.call-start = ((), (), s32[]{:S(2)}) async-start(), calls=%async_computation.1 | async-start | bytes 1179648 | tf_op jit(solution)/shard_map/all_gather | solution.py:263
  10.9 4.3 %collective-permute-start.1 = (f32[1,8,4,128]{3,2,1,0:T(4,128)S(1)}, f32[1,8,4,128]{3,2,1,0:T(4,128)S(1)}, u32[]{:S(2)}, u32[]{:S(2)}) collective-permute-start(f32[1,8,4,128]{3,2,1,0:T(4,128)S(1)} %get-tuple-element.22), channel_id=1, source_target_pairs={{4,0},{8,4},{12,8},{16,12},{20,16},{24,20},{28,24},{5,1},{9,5},{13... | collective-permute-start | bytes 49160 | tf_op jit(solution)/shard_map/ppermute | solution.py:29
  12.2 3.9 %collective-permute-start = (f32[1,8,4,128]{3,2,1,0:T(4,128)S(1)}, f32[1,8,4,128]{3,2,1,0:T(4,128)S(1)}, u32[]{:S(2)}, u32[]{:S(2)}) collective-permute-start(f32[1,8,4,128]{3,2,1,0:T(4,128)S(1)} %get-tuple-element.21), channel_id=1, source_target_pairs={{0,4},{4,8},{8,12},{12,16},{16,20},{20,24},{24,28},{1,5},{5,9},{9,... | collective-permute-start | bytes 49160 | tf_op jit(solution)/shard_map/ppermute | solution.py:27
  16.1 82.2 %copy-start.10 = (s32[512,2]{0,1:T(2,128)S(1)}, s32[512,2]{0,1:T(2,128)}, u32[]{:S(2)}) copy-start(s32[512,2]{0,1:T(2,128)} %param.19) | copy-start | bytes 12292
  16.1 82.2 %copy-start.11 = (s32[512,2]{0,1:T(2,128)S(1)}, s32[512,2]{0,1:T(2,128)}, u32[]{:S(2)}) copy-start(s32[512,2]{0,1:T(2,128)} %param.18) | copy-start | bytes 12292
  16.1 7.0 %collective-permute-start.3 = (f32[10,1,4,128]{3,2,1,0:T(4,128)S(1)}, f32[10,1,4,128]{3,2,1,0:T(4,128)S(1)}, u32[]{:S(2)}, u32[]{:S(2)}) collective-permute-start(f32[10,1,4,128]{3,2,1,0:T(4,128)S(1)} %get-tuple-element.20), channel_id=1, source_target_pairs={{1,0},{2,1},{3,2},{5,4},{6,5},{7,6},{9,8},{10,9},{11,10},{13,12},{... | collective-permute-start | bytes 61448 | tf_op jit(solution)/shard_map/ppermute | solution.py:29
  17.4 7.0 %collective-permute-start.2 = (f32[10,1,4,128]{3,2,1,0:T(4,128)S(1)}, f32[10,1,4,128]{3,2,1,0:T(4,128)S(1)}, u32[]{:S(2)}, u32[]{:S(2)}) collective-permute-start(f32[10,1,4,128]{3,2,1,0:T(4,128)S(1)} %get-tuple-element.19), channel_id=1, source_target_pairs={{0,1},{1,2},{2,3},{4,5},{5,6},{6,7},{8,9},{9,10},{10,11},{12,13},{... | collective-permute-start | bytes 61448 | tf_op jit(solution)/shard_map/ppermute | solution.py:27
  25.6 75.3 %copy-start.8 = (f32[512,3]{0,1:T(4,128)S(1)}, f32[512,3]{0,1:T(4,128)}, u32[]{:S(2)}) copy-start(f32[512,3]{0,1:T(4,128)} %param.16) | copy-start | bytes 18436
  97.6 4.2 %collective-permute-start.5 = (f32[512,3]{0,1:T(4,128)S(1)}, f32[512,3]{0,1:T(4,128)S(1)}, u32[]{:S(2)}, u32[]{:S(2)}) collective-permute-start(f32[512,3]{0,1:T(4,128)S(1)} %copy-done.9), channel_id=1, source_target_pairs={{0,31},{1,0},{2,1},{3,2},{4,3},{5,4},{6,5},{7,6},{8,7},{9,8},{10,9... | collective-permute-start | bytes 18440 | tf_op jit(solution)/shard_map/ppermute | solution.py:265
  97.7 19.7 %collective-permute-start.4 = (f32[512,3,128]{2,0,1:T(8,128)S(1)}, f32[512,3,128]{2,0,1:T(8,128)}, u32[]{:S(2)}, u32[]{:S(2)}) collective-permute-start(f32[512,3,128]{2,0,1:T(8,128)S(1)} %copy-done.1), channel_id=1, source_target_pairs={{0,31},{1,0},{2,1},{3,2},{4,3},{5,4},{6,5},{7,6},{8,7},{9,8},{10,9... | collective-permute-start | bytes 2359304 | tf_op jit(solution)/shard_map/ppermute | solution.py:266
  123.7 60.0 %copy-start = (f32[1024,8,128]{2,1,0:T(8,128)S(1)}, f32[1024,8,128]{2,1,0:T(8,128)}, u32[]{:S(2)}) copy-start(f32[1024,8,128]{2,1,0:T(8,128)} %maximum_maximum_fusion.near_ref) | copy-start | bytes 12582916
  187.0 46.0 %copy-start.2 = (f32[512,8,128]{2,1,0:T(8,128)S(1)}, f32[512,8,128]{2,1,0:T(8,128)}, u32[]{:S(2)}) copy-start(f32[512,8,128]{2,1,0:T(8,128)} %shard_map.124) | copy-start | bytes 6291460
  187.0 46.0 %copy-start.4 = (f32[512,3]{1,0:T(8,128)S(1)}, f32[512,3]{1,0:T(8,128)}, u32[]{:S(2)}) copy-start(f32[512,3]{1,0:T(8,128)} %copy.74) | copy-start | bytes 18436
  238.5 1.0 copy-start.3
Sparse Core Ops, SparseCore 0:
  10.9 72.4 all-gather.2
  97.7 23.3 all-gather.4
